TPU v7x, 256 devices: a whole 4x4x8 slice. The times are simulated.
256 devices in a mesh: comp: 16 (over z, core), pts: 16 (over x, y).
Axes of the slice: x: 4, y: 4, z: 8, core: 2. Of those that a mesh axis runs over, the one named last changes fastest.
Arguments:
- spectra: bfloat16 [3600, 18432], P('comp', 'pts'), may hold values from 0.049804688 to 2
- land_mask: int32 [128, 3600], P('pts'), may hold values from 0 to 1, as said below
- send_rows: int32 [16, 16, 1280], P('pts'), may hold values from 0 to 28799, as said below
- row_counts: int32 [16, 16], replicated, may hold values from 360 to 1280, as said below
- return_index: int32 [16, 13120], P('pts'), may hold values from 0 to 13119, as said below
Outputs:
- owned: bfloat16 [144, 209920], P('comp', 'pts')
Inputs may be any that keep to these rules, and one draw needn't show every extreme that they name: land_mask is 1 exactly at the cells named by the first row_counts[j, d] entries of send_rows[j, d], over all j and d. For k < row_counts[j, d], send_rows[j, d, k] names a cell of band j; all named cells are distinct; entries past the count are 0. For every owner d the sum over j of row_counts[j, d] is 13120. `return_index`: each row is a permutation of 0 to 13119.
All inputs are finite; a program needn't handle non-finite values.
Results may differ from a plain program's by a relative error of at most 0.001.
Values may be sent and summed in bfloat16 or wider, within the bound.
A program may use at most 64 MiB of HBM per device.

v0:
```python
import math

import jax
import jax.numpy as jnp
from jax import lax
from jax.sharding import PartitionSpec as P

ND = 36
ITERS = 4


def extended_2(block, sides, width):
    for axis, dim in sides:
        count = lax.axis_size(axis)
        forward = [(i, i + 1) for i in range(count - 1)]
        backward = [(target, source) for source, target in forward]
        low = lax.ppermute(
            lax.slice_in_dim(block, block.shape[dim] - width, None, axis=dim), axis, forward
        )
        high = lax.ppermute(lax.slice_in_dim(block, 0, width, axis=dim), axis, backward)
        block = jnp.concatenate([low, block, high], axis=dim)
    return block


def lon_parts(values):
    return (jnp.roll(values, 1, axis=-1), values, jnp.roll(values, -1, axis=-1))


def latitude_cosines(first_row, row_total, grid_rows):
    row_ids = (first_row + jnp.arange(row_total)).astype(jnp.float32)
    degrees = 45.0 + 0.1 * (row_ids + 0.5 - 0.5 * grid_rows)
    radians = degrees * (math.pi / 180.0)
    return (jnp.cos(radians), jnp.cos(radians + 0.05 * math.pi / 180.0))


def courant_pairs(comp_ids, grid_rows):
    freq_ids = (comp_ids // ND).astype(jnp.float32)
    dir_ids = (comp_ids % ND).astype(jnp.float32)
    angles = (dir_ids + 0.5) * (2.0 * math.pi / ND)
    top_cos = math.cos((45.0 + 0.05 * grid_rows) * math.pi / 180.0)
    speed_ratio = 0.6 * top_cos * jnp.power(jnp.float32(1.1), -freq_ids)
    return (speed_ratio * jnp.cos(angles), speed_ratio * jnp.sin(angles))


def advance(values, sea_mask, cos_mid, cos_north, east_x, north_y):
    western, centre, eastern = lon_parts(values[:, 1:-1])
    northern = lon_parts(values[:, 2:])[1]
    southern = lon_parts(values[:, :-2])[1]
    mask_west, mask_centre, mask_east = lon_parts(sea_mask[1:-1])
    mask_north = lon_parts(sea_mask[2:])[1]
    mask_south = lon_parts(sea_mask[:-2])[1]
    inner_cos = cos_mid[1:-1][None, :, None]
    courant_x = east_x[:, None, None] / inner_cos
    ahead_x = jnp.maximum(courant_x, 0.0)
    behind = jnp.minimum(courant_x, 0.0)
    flux_east = (ahead_x * centre + behind * eastern) * (mask_centre * mask_east)
    flux_west = (ahead_x * western + behind * centre) * (mask_west * mask_centre)
    across = north_y[:, None, None]
    upward = jnp.maximum(across, 0.0)
    downward = jnp.minimum(across, 0.0)
    flux_north = (
        (upward * centre + downward * northern)
        * (mask_centre * mask_north)
        * cos_north[1:-1][None, :, None]
    )
    flux_south = (
        (upward * southern + downward * centre)
        * (mask_south * mask_centre)
        * cos_north[:-2][None, :, None]
    )
    updated = mask_centre * (
        centre - (flux_east - flux_west) - (flux_north - flux_south) / inner_cos
    )
    return (updated, mask_centre)


def local(spectra, land_mask, send_rows, row_counts, return_index):
    comp_count = lax.axis_size("comp")
    pts_count = lax.axis_size("pts")
    comp_here = lax.axis_index("comp")
    pts_here = lax.axis_index("pts")
    band_rows = land_mask.shape[0]
    lon_cells = land_mask.shape[1]
    grid_rows = band_rows * pts_count
    lon_block = spectra.shape[0]
    total_comps = spectra.shape[1] // band_rows
    comp_block = total_comps // comp_count
    rim_depth = 1
    mask_rows = extended_2(land_mask, (("pts", 0),), ITERS).astype(jnp.float32)
    pieces = spectra.reshape(lon_block, band_rows, comp_count, comp_block)
    arrived = lax.all_to_all(pieces, "comp", split_axis=2, concat_axis=0, tiled=True)[:, :, 0, :]
    arrived = jnp.transpose(arrived, (2, 1, 0))
    comp_ids = comp_here * comp_block + jnp.arange(comp_block, dtype=jnp.int32)
    values = arrived.astype(jnp.float32)
    east_x, north_y = courant_pairs(comp_ids, grid_rows)
    for _ in range(ITERS // rim_depth):
        sea_mask = mask_rows[ITERS - rim_depth : ITERS + band_rows + rim_depth]
        extended = extended_2(values, (("pts", 1),), rim_depth)
        cos_mid, cos_north = latitude_cosines(
            pts_here * band_rows - rim_depth, band_rows + 2 * rim_depth, grid_rows
        )
        extended, sea_mask = advance(extended, sea_mask, cos_mid, cos_north, east_x, north_y)
        cos_mid = cos_mid[1:-1]
        cos_north = cos_north[1:-1]
        values = extended
    component_view = values.astype(jnp.bfloat16)
    cell_table = component_view.reshape(comp_block, band_rows * lon_cells).T
    route_rows = send_rows[0]
    capacity = route_rows.shape[1]
    outgoing = jnp.take(cell_table, route_rows.reshape(-1), axis=0).reshape(
        pts_count, capacity, comp_block
    )
    received = lax.all_to_all(outgoing, "pts", split_axis=0, concat_axis=0, tiled=True).reshape(
        pts_count * capacity, comp_block
    )
    counts_in = lax.dynamic_slice_in_dim(row_counts, pts_here, 1, 1)[:, 0]
    offsets = jnp.cumsum(counts_in) - counts_in
    picked = return_index[0]
    source = jnp.sum((picked[:, None] >= offsets[None, :]).astype(jnp.int32), axis=1) - 1
    start_row = jnp.sum(
        jnp.where(
            source[:, None] == jnp.arange(pts_count, dtype=jnp.int32)[None, :], offsets[None, :], 0
        ),
        axis=1,
    )
    slot_ids = source * capacity + picked - start_row
    return jnp.take(received, slot_ids, axis=0).T


def solution(mesh):
    placed = (P("comp", "pts"), P("pts", None), P("pts", None, None), P(), P("pts", None))
    return jax.shard_map(
        local, mesh=mesh, in_specs=placed, out_specs=P("comp", "pts"), check_vma=False
    )
```

profile of v0, /device:TPU:32, one launch (start us, length us, event | category | flops | bytes accessed | tf_op | source)
XLA Modules:
  0.0 231.9 jit_solution(7960250178626434973)
XLA Ops:
  1.0 3.5 %collective-permute-start = (s32[4,3600]{1,0:T(4,128)S(1)}, s32[4,3600]{1,0:T(4,128)S(1)}, u32[]{:S(2)}, u32[]{:S(2)}) collective-permute-start(s32[4,3600]{1,0:T(4,128)S(1)} %get-tuple-element.38), channel_id=1, source_target_pairs={{0,1},{1,2},{2,3},{3,4},{4,5},{5,6},{6,7},{7,8},{8,9},{9,10},{10,1... | collective-permute-start | bytes 172808 | tf_op jit(solution)/shard_map/ppermute | solution.py:17
  4.5 1.3 collective-permute-start.1
  5.8 1.3 copy.19
  7.4 1.2 copy.20
  8.6 8.7 %all-to-all-start = ((bf16[225,8,16,9]{0,1,3,2:T(8,128)(2,1)}), bf16[225,8,16,9]{0,1,3,2:T(8,128)(2,1)S(1)}, u32[]{:S(2)}, u32[]{:S(2)}) async-start(bf16[225,8,16,9]{0,1,3,2:T(8,128)(2,1)} %copy.20), calls=%async_computation | async-start | bytes 1179648 | tf_op jit(solution)/shard_map/all_to_all | solution.py:91
  19.6 13.2 %all-to-all-done = bf16[225,8,16,9]{0,1,3,2:T(8,128)(2,1)S(1)} async-done(((bf16[225,8,16,9]{0,1,3,2:T(8,128)(2,1)}), bf16[225,8,16,9]{0,1,3,2:T(8,128)(2,1)S(1)}, u32[]{:S(2)}, u32[]{:S(2)}) %all-to-all-start) | async-done | bytes 518432 | tf_op jit(solution)/shard_map/all_to_all | solution.py:91
  34.4 1.3 collective-permute-start.2
  35.7 5.2 %collective-permute-start.3 = (f32[9,1,3600]{2,1,0:T(1,128)S(1)}, f32[9,1,3600]{2,1,0:T(1,128)S(1)}, u32[]{:S(2)}, u32[]{:S(2)}) collective-permute-start(f32[9,1,3600]{2,1,0:T(1,128)S(1)} %get-tuple-element.28), channel_id=1, source_target_pairs={{0,1},{1,2},{2,3},{3,4},{4,5},{5,6},{6,7},{7,8},{8,9},{9,10},{10,1... | collective-permute-start | bytes 388808 | tf_op jit(solution)/shard_map/ppermute | solution.py:17
  41.0 1.8 collective-permute-done.2
  42.8 1.2 collective-permute-done.3
  44.0 1.4 fusion.68
  45.9 1.3 collective-permute-start.4
  47.2 5.0 %collective-permute-start.5 = (f32[9,1,3600]{2,1,0:T(1,128)S(1)}, f32[9,1,3600]{2,1,0:T(1,128)S(1)}, u32[]{:S(2)}, u32[]{:S(2)}) collective-permute-start(f32[9,1,3600]{2,1,0:T(1,128)S(1)} %get-tuple-element.22), channel_id=1, source_target_pairs={{0,1},{1,2},{2,3},{3,4},{4,5},{5,6},{6,7},{7,8},{8,9},{9,10},{10,1... | collective-permute-start | bytes 388808 | tf_op jit(solution)/shard_map/ppermute | solution.py:17
  53.3 1.5 collective-permute-done.5
  54.7 1.4 fusion.69
  56.6 1.3 collective-permute-start.6
  57.9 5.0 %collective-permute-start.7 = (f32[9,1,3600]{2,1,0:T(1,128)S(1)}, f32[9,1,3600]{2,1,0:T(1,128)S(1)}, u32[]{:S(2)}, u32[]{:S(2)}) collective-permute-start(f32[9,1,3600]{2,1,0:T(1,128)S(1)} %get-tuple-element.16), channel_id=1, source_target_pairs={{0,1},{1,2},{2,3},{3,4},{4,5},{5,6},{6,7},{7,8},{8,9},{9,10},{10,1... | collective-permute-start | bytes 388808 | tf_op jit(solution)/shard_map/ppermute | solution.py:17
  63.9 1.5 collective-permute-done.7
  65.4 1.4 fusion.70
  67.3 1.3 collective-permute-start.8
  68.6 5.2 %collective-permute-start.9 = (f32[9,1,3600]{2,1,0:T(1,128)S(1)}, f32[9,1,3600]{2,1,0:T(1,128)S(1)}, u32[]{:S(2)}, u32[]{:S(2)}) collective-permute-start(f32[9,1,3600]{2,1,0:T(1,128)S(1)} %get-tuple-element.10), channel_id=1, source_target_pairs={{0,1},{1,2},{2,3},{3,4},{4,5},{5,6},{6,7},{7,8},{8,9},{9,10},{10,1... | collective-permute-start | bytes 388808 | tf_op jit(solution)/shard_map/ppermute | solution.py:17
  74.7 1.5 collective-permute-done.9
  76.1 1.4 multiply_convert_fusion
  77.5 5.2 %copy.22 = bf16[9,8,3600]{0,2,1:T(8,128)(2,1)} copy(bf16[9,8,3600]{2,1,0:T(8,128)(2,1)S(1)} %multiply_convert_fusion) | data formatting | bytes 1036800 | tf_op jit(solution)/shard_map/convert_element_type | solution.py:106
  82.8 73.2 %gather_fusion = bf16[20480,9]{1,0:T(8,128)(2,1)} fusion(bf16[28800,9]{1,0:T(8,128)(2,1)} %bitcast.33, s32[20480]{0:T(1024)S(1)} %broadcast_clamp_fusion), kind=kCustom, calls=%fused_computation | custom fusion | bytes 819200 | tf_op jit(solution)/shard_map/jit(_take)/gather | solution.py:110
  156.0 4.1 %copy.23 = bf16[16,1280,9]{1,2,0:T(8,128)(2,1)S(1)} copy(bf16[16,1280,9]{2,1,0:T(8,128)(2,1)} %bitcast.35) | data formatting | bytes 737280 | tf_op jit(solution)/shard_map/jit(_take)/gather | solution.py:110
  161.1 16.5 %all-to-all-start.1 = ((bf16[16,1280,9]{1,2,0:T(8,128)(2,1)}), bf16[16,1280,9]{1,2,0:T(8,128)(2,1)S(1)}, u32[]{:S(2)}, u32[]{:S(2)}) async-start(bf16[16,1280,9]{1,2,0:T(8,128)(2,1)} %broadcast_select_fusion), calls=%async_computation.1 | async-start | bytes 1310720 | tf_op jit(solution)/shard_map/all_to_all | solution.py:113
  177.6 10.8 %all-to-all-done.1 = bf16[16,1280,9]{1,2,0:T(8,128)(2,1)S(1)} async-done(((bf16[16,1280,9]{1,2,0:T(8,128)(2,1)}), bf16[16,1280,9]{1,2,0:T(8,128)(2,1)S(1)}, u32[]{:S(2)}, u32[]{:S(2)}) %all-to-all-start.1) | async-done | bytes 368672 | tf_op jit(solution)/shard_map/all_to_all | solution.py:113
  188.3 3.7 %copy.24 = bf16[16,1280,9]{2,1,0:T(8,128)(2,1)} copy(bf16[16,1280,9]{1,2,0:T(8,128)(2,1)S(1)} %all-to-all-done.1) | data formatting | bytes 737280 | tf_op jit(solution)/shard_map/all_to_all | solution.py:113
  192.0 28.5 %gather_fusion.1 = bf16[13120,9]{1,0:T(8,128)(2,1)} fusion(bf16[20480,9]{1,0:T(8,128)(2,1)} %bitcast.34, s32[13312]{0:T(1024)S(1)} %pad_clamp_fusion), kind=kCustom, calls=%fused_computation.1 | custom fusion | bytes 524800 | tf_op jit(solution)/shard_map/jit(_take)/gather | solution.py:127
  220.5 8.2 %select_bitcast_fusion = bf16[9,13120]{0,1:T(8,128)(2,1)S(1)} fusion(bf16[13120,9]{1,0:T(8,128)(2,1)} %gather_fusion.1, pred[13120]{0:T(1024)(128)(4,1)S(1)} %compare_and_fusion.1), kind=kLoop, calls=%fused_computation.2 | loop fusion | flops 118080 | bytes 485440 | tf_op jit(solution)/shard_map/jit(_take)/select_n | solution.py:127
  228.7 3.2 %copy.25 = bf16[9,13120]{1,0:T(8,128)(2,1)} copy(bf16[9,13120]{0,1:T(8,128)(2,1)S(1)} %select_bitcast_fusion) | data formatting | bytes 472320 | tf_op jit(solution)/shard_map/jit(_take)/select_n | solution.py:127
  (56 shorter events, 10.6 us)
Async XLA Ops:
  1.0 18.2 %collective-permute-start = (s32[4,3600]{1,0:T(4,128)S(1)}, s32[4,3600]{1,0:T(4,128)S(1)}, u32[]{:S(2)}, u32[]{:S(2)}) collective-permute-start(s32[4,3600]{1,0:T(4,128)S(1)} %get-tuple-element.38), channel_id=1, source_target_pairs={{0,1},{1,2},{2,3},{3,4},{4,5},{5,6},{6,7},{7,8},{8,9},{9,10},{10,1... | collective-permute-start | bytes 172808 | tf_op jit(solution)/shard_map/ppermute | solution.py:17
  4.5 14.7 %collective-permute-start.1 = (s32[4,3600]{1,0:T(4,128)S(1)}, s32[4,3600]{1,0:T(4,128)S(1)}, u32[]{:S(2)}, u32[]{:S(2)}) collective-permute-start(s32[4,3600]{1,0:T(4,128)S(1)} %get-tuple-element.39), channel_id=1, source_target_pairs={{1,0},{2,1},{3,2},{4,3},{5,4},{6,5},{7,6},{8,7},{9,8},{10,9},{11,1... | collective-permute-start | bytes 172808 | tf_op jit(solution)/shard_map/ppermute | solution.py:20
  7.4 10.2 %copy-start.1 = (s32[1,16,1280]{2,1,0:T(8,128)S(1)}, s32[1,16,1280]{2,1,0:T(8,128)}, u32[]{:S(2)}) copy-start(s32[1,16,1280]{2,1,0:T(8,128)} %param.7) | copy-start | bytes 245764
  8.6 9.3 %copy-start.3 = (s32[16,16]{1,0:T(8,128)S(1)}, s32[16,16]{1,0:T(8,128)}, u32[]{:S(2)}) copy-start(s32[16,16]{1,0:T(8,128)} %param.8) | copy-start | bytes 3076
  8.6 9.6 %copy-start.2 = (s32[1,13120]{1,0:T(1,128)S(1)}, s32[1,13120]{1,0:T(1,128)}, u32[]{:S(2)}) copy-start(s32[1,13120]{1,0:T(1,128)} %param.9) | copy-start | bytes 157444
  8.6 10.6 %copy-start = (s32[8,3600]{1,0:T(8,128)S(1)}, s32[8,3600]{1,0:T(8,128)}, u32[]{:S(2)}) copy-start(s32[8,3600]{1,0:T(8,128)} %param.6) | copy-start | bytes 345604
  8.6 24.2 %all-to-all-start = ((bf16[225,8,16,9]{0,1,3,2:T(8,128)(2,1)}), bf16[225,8,16,9]{0,1,3,2:T(8,128)(2,1)S(1)}, u32[]{:S(2)}, u32[]{:S(2)}) async-start(bf16[225,8,16,9]{0,1,3,2:T(8,128)(2,1)} %copy.20), calls=%async_computation | async-start | bytes 1179648 | tf_op jit(solution)/shard_map/all_to_all | solution.py:91
  34.4 8.4 %collective-permute-start.2 = (f32[9,1,3600]{2,1,0:T(1,128)S(1)}, f32[9,1,3600]{2,1,0:T(1,128)S(1)}, u32[]{:S(2)}, u32[]{:S(2)}) collective-permute-start(f32[9,1,3600]{2,1,0:T(1,128)S(1)} %get-tuple-element.27), channel_id=1, source_target_pairs={{1,0},{2,1},{3,2},{4,3},{5,4},{6,5},{7,6},{8,7},{9,8},{10,9},{11,1... | collective-permute-start | bytes 388808 | tf_op jit(solution)/shard_map/ppermute | solution.py:20
  35.7 8.3 %collective-permute-start.3 = (f32[9,1,3600]{2,1,0:T(1,128)S(1)}, f32[9,1,3600]{2,1,0:T(1,128)S(1)}, u32[]{:S(2)}, u32[]{:S(2)}) collective-permute-start(f32[9,1,3600]{2,1,0:T(1,128)S(1)} %get-tuple-element.28), channel_id=1, source_target_pairs={{0,1},{1,2},{2,3},{3,4},{4,5},{5,6},{6,7},{7,8},{8,9},{9,10},{10,1... | collective-permute-start | bytes 388808 | tf_op jit(solution)/shard_map/ppermute | solution.py:17
  45.9 7.4 %collective-permute-start.4 = (f32[9,1,3600]{2,1,0:T(1,128)S(1)}, f32[9,1,3600]{2,1,0:T(1,128)S(1)}, u32[]{:S(2)}, u32[]{:S(2)}) collective-permute-start(f32[9,1,3600]{2,1,0:T(1,128)S(1)} %get-tuple-element.21), channel_id=1, source_target_pairs={{1,0},{2,1},{3,2},{4,3},{5,4},{6,5},{7,6},{8,7},{9,8},{10,9},{11,1... | collective-permute-start | bytes 388808 | tf_op jit(solution)/shard_map/ppermute | solution.py:20
  47.2 7.5 %collective-permute-start.5 = (f32[9,1,3600]{2,1,0:T(1,128)S(1)}, f32[9,1,3600]{2,1,0:T(1,128)S(1)}, u32[]{:S(2)}, u32[]{:S(2)}) collective-permute-start(f32[9,1,3600]{2,1,0:T(1,128)S(1)} %get-tuple-element.22), channel_id=1, source_target_pairs={{0,1},{1,2},{2,3},{3,4},{4,5},{5,6},{6,7},{7,8},{8,9},{9,10},{10,1... | collective-permute-start | bytes 388808 | tf_op jit(solution)/shard_map/ppermute | solution.py:17
  56.6 7.3 %collective-permute-start.6 = (f32[9,1,3600]{2,1,0:T(1,128)S(1)}, f32[9,1,3600]{2,1,0:T(1,128)S(1)}, u32[]{:S(2)}, u32[]{:S(2)}) collective-permute-start(f32[9,1,3600]{2,1,0:T(1,128)S(1)} %get-tuple-element.15), channel_id=1, source_target_pairs={{1,0},{2,1},{3,2},{4,3},{5,4},{6,5},{7,6},{8,7},{9,8},{10,9},{11,1... | collective-permute-start | bytes 388808 | tf_op jit(solution)/shard_map/ppermute | solution.py:20
  57.9 7.5 %collective-permute-start.7 = (f32[9,1,3600]{2,1,0:T(1,128)S(1)}, f32[9,1,3600]{2,1,0:T(1,128)S(1)}, u32[]{:S(2)}, u32[]{:S(2)}) collective-permute-start(f32[9,1,3600]{2,1,0:T(1,128)S(1)} %get-tuple-element.16), channel_id=1, source_target_pairs={{0,1},{1,2},{2,3},{3,4},{4,5},{5,6},{6,7},{7,8},{8,9},{9,10},{10,1... | collective-permute-start | bytes 388808 | tf_op jit(solution)/shard_map/ppermute | solution.py:17
  67.3 7.3 %collective-permute-start.8 = (f32[9,1,3600]{2,1,0:T(1,128)S(1)}, f32[9,1,3600]{2,1,0:T(1,128)S(1)}, u32[]{:S(2)}, u32[]{:S(2)}) collective-permute-start(f32[9,1,3600]{2,1,0:T(1,128)S(1)} %get-tuple-element.9), channel_id=1, source_target_pairs={{1,0},{2,1},{3,2},{4,3},{5,4},{6,5},{7,6},{8,7},{9,8},{10,9},{11,1... | collective-permute-start | bytes 388808 | tf_op jit(solution)/shard_map/ppermute | solution.py:20
  68.6 7.5 %collective-permute-start.9 = (f32[9,1,3600]{2,1,0:T(1,128)S(1)}, f32[9,1,3600]{2,1,0:T(1,128)S(1)}, u32[]{:S(2)}, u32[]{:S(2)}) collective-permute-start(f32[9,1,3600]{2,1,0:T(1,128)S(1)} %get-tuple-element.10), channel_id=1, source_target_pairs={{0,1},{1,2},{2,3},{3,4},{4,5},{5,6},{6,7},{7,8},{8,9},{9,10},{10,1... | collective-permute-start | bytes 388808 | tf_op jit(solution)/shard_map/ppermute | solution.py:17
  161.1 27.3 %all-to-all-start.1 = ((bf16[16,1280,9]{1,2,0:T(8,128)(2,1)}), bf16[16,1280,9]{1,2,0:T(8,128)(2,1)S(1)}, u32[]{:S(2)}, u32[]{:S(2)}) async-start(bf16[16,1280,9]{1,2,0:T(8,128)(2,1)} %broadcast_select_fusion), calls=%async_computation.1 | async-start | bytes 1310720 | tf_op jit(solution)/shard_map/all_to_all | solution.py:113
where the time goes:
time: 235 us; the launch traced here: 232 us
  local copies, waits for them, and re-layouts  125 us (53%)
  starting transfers between devices  55.5 us (24%)
  waiting for transfers between devices  34.1 us (15%)
  other arithmetic  16.5 us (7%)
    gather x2, local copies, waits for them, and re-layouts, local(): jnp.take(cell_table, route_rows.reshape(-1), axis=0)  77.3 us
    gather x1, local copies, waits for them, and re-layouts, local(): return jnp.take(received, slot_ids, axis=0).T  28.5 us
    ppermute x5, starting transfers between devices, extended_2(): lax.ppermute(lax.slice_in_dim(block, block.shape[dim] - width, None, axis...  23.8 us
    all_to_all x1, starting transfers between devices, local(): lax.all_to_all(outgoing, 'pts', split_axis=0, concat_axis=0, tiled=True)  16.5 us
    all_to_all x1, waiting for transfers between devices, local(): lax.all_to_all(pieces, 'comp', split_axis=2, concat_axis=0, tiled=True)  13.2 us
    all_to_all x1, waiting for transfers between devices, local(): lax.all_to_all(outgoing, 'pts', split_axis=0, concat_axis=0, tiled=True)  10.8 us
    all_to_all x1, starting transfers between devices, local(): lax.all_to_all(pieces, 'comp', split_axis=2, concat_axis=0, tiled=True)  8.72 us
    select_n x2, other arithmetic, local(): return jnp.take(received, slot_ids, axis=0).T  8.44 us
  transfers between devices with their start and end apart: 12, of which 10 were waited for; matrix products, arithmetic and copies ran while one was open for 2% of the time, Pallas kernels for 0%

commit v1 on v0

v1 whole, which is shorter than its diff:
```python
import functools
import math

import jax
import jax.numpy as jnp
from jax import lax
from jax.experimental import pallas as pl
from jax.experimental.pallas import tpu as pltpu
from jax.sharding import PartitionSpec as P

ND = 36
ITERS = 4
LANES = 128
CB = 9
ROWS = 8
OWN = ITERS * CB
LON = 3600
LB = 225
SEG = 80
NB = 16
PAD = 8
GROUPS = 14
CAP = 1280
CAP_ROWS = 96
SLOT_ROWS = 1024
SLOT_GROUPS = 13
F32 = jnp.float32
BF16 = jnp.bfloat16


def iota(shape, dim):
    return lax.broadcasted_iota(jnp.int32, shape, dim)


def one_hot(cond):
    return jnp.where(cond, 1.0, 0.0).astype(BF16)


def mm(a, b):
    return jnp.dot(a, b, preferred_element_type=F32)


def propagate_kernel(
    x_ref, mask_ref, coef_ref, out_ref,
    sendbuf, piece, hsend, hrecv, ymid, mprev, mnext, mstack, mexp, mdown, kbuf, va, vb,
    s_send, s_recv, h_send, h_recv, m_send, m_recv, l_sem,
):
    c = lax.axis_index("comp")
    j = lax.axis_index("pts")
    nxt = lax.rem(j + 1, NB)
    prv = lax.rem(j + NB - 1, NB)
    quad = lax.rem(c, 4)
    north = quad < 2
    east = jnp.logical_or(quad == 0, quad == 3)
    down = jnp.where(north, nxt, prv)

    barrier = pltpu.get_barrier_semaphore()
    for s in range(1, NB):
        pl.semaphore_signal(
            barrier, inc=1, device_id={"comp": lax.rem(c + s, NB)}, device_id_type=pl.DeviceIdType.MESH
        )
    for other in (nxt, prv):
        pl.semaphore_signal(barrier, inc=1, device_id={"pts": other}, device_id_type=pl.DeviceIdType.MESH)

    ymid[LB : 3 * SEG, :] = jnp.zeros((3 * SEG - LB, LANES), F32)
    m_id = iota((ROWS * NB * CB, LANES), 0)
    lane = iota((1, LANES), 1)
    pos = lane // CB
    lane_s = iota((SEG, LANES), 1)
    x = x_ref[...]
    for t in range(NB):
        row = pos if t % 4 < 2 else ROWS - 1 - pos
        want = jnp.where(lane < ROWS * CB, row * (NB * CB) + t * CB + lane - pos * CB, -1)
        ymid[0:LB, :] = mm(x, one_hot(m_id == want))
        y0 = ymid[0:SEG, :]
        y1 = pltpu.roll(ymid[SEG : 2 * SEG, :], 72, 1)
        y2 = pltpu.roll(ymid[2 * SEG : 3 * SEG, :], 16, 1)
        sendbuf[t, :, 0:LANES] = jnp.where(lane_s < 72, y0, y1).astype(BF16)
        sendbuf[t, :, LANES : 2 * LANES] = jnp.where(lane_s < 16, y1, y2).astype(BF16)

    pl.semaphore_wait(barrier, NB + 1)

    copies = []
    for s in range(1, NB):
        to = lax.rem(c + s, NB)
        copies.append(
            pltpu.make_async_remote_copy(
                src_ref=sendbuf.at[to], dst_ref=piece.at[c], send_sem=s_send.at[to], recv_sem=s_recv.at[c],
                device_id={"comp": to}, device_id_type=pl.DeviceIdType.MESH,
            )
        )
        copies[-1].start()
    m_up = pltpu.make_async_remote_copy(
        src_ref=mask_ref, dst_ref=mprev, send_sem=m_send.at[0], recv_sem=m_recv.at[0],
        device_id={"pts": nxt}, device_id_type=pl.DeviceIdType.MESH,
    )
    m_up.start()
    m_dn = pltpu.make_async_remote_copy(
        src_ref=mask_ref, dst_ref=mnext, send_sem=m_send.at[1], recv_sem=m_recv.at[1],
        device_id={"pts": prv}, device_id_type=pl.DeviceIdType.MESH,
    )
    m_dn.start()
    own = pltpu.make_async_copy(sendbuf.at[c], piece.at[c], l_sem)
    own.start()

    m_up.wait()
    m_dn.wait()
    mstack[0:ROWS, :] = jnp.where(j > 0, mprev[...], 0).astype(F32)
    mstack[ROWS : 2 * ROWS, :] = mask_ref[...].astype(F32)
    mstack[2 * ROWS : 3 * ROWS, :] = jnp.where(j < NB - 1, mnext[...], 0).astype(F32)
    g_id = iota((3 * ROWS, LANES), 0)
    l_id = iota((3 * ROWS, LANES), 1)
    rr = l_id // CB
    live = rr < ROWS + ITERS
    e_here = one_hot(jnp.logical_and(live, g_id == jnp.where(north, rr + 4, 19 - rr)))
    e_down = one_hot(jnp.logical_and(live, g_id == jnp.where(north, rr + 5, 18 - rr)))
    e_both = jnp.concatenate([e_here, e_down], axis=1)
    stack = mstack[...].astype(BF16)
    both = lax.dot_general(stack, e_both, (((0,), (0,)), ((), ())), preferred_element_type=F32)
    mexp[PAD : PAD + LON, :] = both[:, :LANES]
    mdown[...] = both[:, LANES:]
    mexp[PAD - 1 : PAD, :] = mexp[PAD + LON - 1 : PAD + LON, :]
    mexp[PAD + LON : PAD + LON + 1, :] = mexp[PAD : PAD + 1, :]
    ax = coef_ref[0:1, :]
    ay = coef_ref[1:2, :]
    ad = coef_ref[2:3, :]
    step_rows = 120
    for i in range(LON // step_rows):
        a = PAD + i * step_rows
        m = mexp[a : a + step_rows, :]
        lon_down = jnp.where(
            east, mexp[a + 1 : a + 1 + step_rows, :], mexp[a - 1 : a - 1 + step_rows, :]
        )
        kbuf[i * step_rows : (i + 1) * step_rows, :] = m * (
            1.0 - ax * lon_down - ad * mdown[i * step_rows : (i + 1) * step_rows, :]
        )

    src = iota((2 * LANES, LANES), 0)
    dst = iota((2 * LANES, LANES), 1)
    seg = dst // OWN
    h_pack = one_hot(
        jnp.logical_and(seg < 3, src == seg * (ROWS * CB) + (ROWS - ITERS) * CB + dst - seg * OWN)
    )
    hops = []
    for b in range(NB):

        @pl.when(b == c)
        def _():
            own.wait()

        @pl.when(b != c)
        def _():
            pltpu.make_async_remote_copy(
                src_ref=sendbuf.at[b], dst_ref=piece.at[b], send_sem=s_send.at[b], recv_sem=s_recv.at[b],
                device_id={"comp": b}, device_id_type=pl.DeviceIdType.MESH,
            ).wait_recv()

        hsend[b] = mm(piece[b], h_pack).astype(BF16)
        hops.append(
            pltpu.make_async_remote_copy(
                src_ref=hsend.at[b], dst_ref=hrecv.at[b], send_sem=h_send.at[b], recv_sem=h_recv.at[b],
                device_id={"pts": down}, device_id_type=pl.DeviceIdType.MESH,
            )
        )
        hops[-1].start()

    u_src = iota((2 * LANES, 3 * LANES), 0)
    u_dst = iota((2 * LANES, 3 * LANES), 1)
    u_seg = u_dst // LANES
    u_lane = u_dst - u_seg * LANES
    own_lane = jnp.logical_and(u_lane >= OWN, u_lane < OWN + ROWS * CB)
    unpack = one_hot(jnp.logical_and(own_lane, u_src == u_seg * (ROWS * CB) + u_lane - OWN))
    hu_src = iota((LANES, 3 * LANES), 0)
    hu_dst = iota((LANES, 3 * LANES), 1)
    hu_seg = hu_dst // LANES
    hu_lane = hu_dst - hu_seg * LANES
    h_unpack = one_hot(jnp.logical_and(hu_lane < OWN, hu_src == hu_seg * OWN + hu_lane))
    for b in range(NB):
        hops[b].wait_recv()
        full = mm(piece[b], unpack) + mm(hrecv[b], h_unpack)
        for t in range(3):
            size = min(SEG, LB - t * SEG)
            a = PAD + b * LB + t * SEG
            va[a : a + size, :] = full[:size, t * LANES : (t + 1) * LANES] * mexp[a : a + size, :]

    for it in range(ITERS):
        v, w = (va, vb) if it % 2 == 0 else (vb, va)
        v[PAD - 1 : PAD, :] = v[PAD + LON - 1 : PAD + LON, :]
        v[PAD + LON : PAD + LON + 1, :] = v[PAD : PAD + 1, :]
        for i in range(LON // step_rows):
            a = PAD + i * step_rows
            k = i * step_rows
            here = v[a : a + step_rows, :]
            side = jnp.where(east, v[a - 1 : a - 1 + step_rows, :], v[a + 1 : a + 1 + step_rows, :])
            new = kbuf[k : k + step_rows, :] * here + mexp[a : a + step_rows, :] * (
                ax * side + ay * pltpu.roll(here, CB, 1)
            )
            if it < ITERS - 1:
                w[a : a + step_rows, :] = new
            else:
                out_ref[k : k + step_rows, :] = new.astype(BF16)

    for copy in copies:
        copy.wait_send()
    for hop in hops:
        hop.wait_send()


def propagate(x, mask, coef):
    dma = pltpu.SemaphoreType.DMA
    vmem = pl.BlockSpec(memory_space=pltpu.VMEM)
    wrapped = PAD + LON + 8
    return pl.pallas_call(
        propagate_kernel,
        out_shape=jax.ShapeDtypeStruct((LON, LANES), BF16),
        in_specs=[vmem, vmem, vmem],
        out_specs=vmem,
        scratch_shapes=[
            pltpu.VMEM((NB, SEG, 2 * LANES), BF16),
            pltpu.VMEM((NB, SEG, 2 * LANES), BF16),
            pltpu.VMEM((NB, SEG, LANES), BF16),
            pltpu.VMEM((NB, SEG, LANES), BF16),
            pltpu.VMEM((3 * SEG, LANES), F32),
            pltpu.VMEM((ROWS, LON), jnp.int32),
            pltpu.VMEM((ROWS, LON), jnp.int32),
            pltpu.VMEM((3 * ROWS, LON), F32),
            pltpu.VMEM((wrapped, LANES), F32),
            pltpu.VMEM((LON, LANES), F32),
            pltpu.VMEM((LON, LANES), F32),
            pltpu.VMEM((wrapped, LANES), F32),
            pltpu.VMEM((wrapped, LANES), F32),
            dma((NB,)), dma((NB,)), dma((NB,)), dma((NB,)), dma((2,)), dma((2,)), dma,
        ],
        compiler_params=pltpu.CompilerParams(
            collective_id=0, has_side_effects=True, vmem_limit_bytes=40 << 20
        ),
        name="propagate",
    )(x, mask, coef)


def select_kernel(rows_ref, idx_ref, v_ref, out_ref, tab, stage):
    src = iota((LANES, 2 * LANES), 0)
    dst = iota((LANES, 2 * LANES), 1)
    half = dst // LANES
    lane2 = dst - half * LANES
    chunk = 240
    for pair in range(ROWS // 2):
        spread = one_hot(
            jnp.logical_and(
                lane2 < GROUPS * CB, src == OWN + (2 * pair + half) * CB + lane2 - (lane2 // CB) * CB
            )
        )

        def fill(i, _, spread=spread, pair=pair):
            a = pl.multiple_of(i * chunk, chunk)
            both = mm(v_ref[pl.ds(a, chunk), :], spread)
            tab[pl.ds(2 * pair * LON + a, chunk), :] = both[:, :LANES]
            tab[pl.ds((2 * pair + 1) * LON + a, chunk), :] = both[:, LANES:]
            return 0

        lax.fori_loop(0, LON // chunk, fill, 0)

    lane = iota((1, LANES), 1)
    unroll = 2

    def owner(d, _):
        base = d * (CAP_ROWS * GROUPS)

        def block(q, _):
            for u in range(unroll):
                r = q * unroll + u
                e = base + r * GROUPS
                acc = tab[pl.ds(idx_ref[e], 1), :]
                for g in range(1, GROUPS):
                    acc = jnp.where(lane >= CB * g, tab[pl.ds(idx_ref[e + g], 1), :], acc)
                stage[pl.ds(r, 1), :] = acc
            return 0

        lax.fori_loop(0, rows_ref[d], block, 0)
        out_ref[d] = stage[...].astype(BF16)
        return 0

    lax.fori_loop(0, NB, owner, 0)


def select_cells(rows, idx, v):
    smem = pl.BlockSpec(memory_space=pltpu.SMEM)
    vmem = pl.BlockSpec(memory_space=pltpu.VMEM)
    return pl.pallas_call(
        select_kernel,
        out_shape=jax.ShapeDtypeStruct((NB, CAP_ROWS, LANES), BF16),
        in_specs=[smem, smem, vmem],
        out_specs=vmem,
        scratch_shapes=[pltpu.VMEM((ROWS * LON, LANES), F32), pltpu.VMEM((CAP_ROWS, LANES), F32)],
        compiler_params=pltpu.CompilerParams(vmem_limit_bytes=40 << 20),
        name="select_cells",
    )(rows, idx, v)


def exchange_kernel(src_ref, out_ref, send, recv, l_sem):
    j = lax.axis_index("pts")
    barrier = pltpu.get_barrier_semaphore()
    for s in range(1, NB):
        pl.semaphore_signal(
            barrier, inc=1, device_id={"pts": lax.rem(j + s, NB)}, device_id_type=pl.DeviceIdType.MESH
        )
    own = pltpu.make_async_copy(src_ref.at[j], out_ref.at[j], l_sem)
    own.start()
    pl.semaphore_wait(barrier, NB - 1)
    copies = []
    for s in range(1, NB):
        to = lax.rem(j + s, NB)
        copies.append(
            pltpu.make_async_remote_copy(
                src_ref=src_ref.at[to], dst_ref=out_ref.at[j], send_sem=send.at[s], recv_sem=recv.at[s],
                device_id={"pts": to}, device_id_type=pl.DeviceIdType.MESH,
            )
        )
        copies[-1].start()
    own.wait()
    for copy in copies:
        copy.wait()


def exchange(outgoing):
    vmem = pl.BlockSpec(memory_space=pltpu.VMEM)
    return pl.pallas_call(
        exchange_kernel,
        out_shape=jax.ShapeDtypeStruct(outgoing.shape, outgoing.dtype),
        in_specs=[vmem],
        out_specs=vmem,
        scratch_shapes=[
            pltpu.SemaphoreType.DMA((NB,)), pltpu.SemaphoreType.DMA((NB,)), pltpu.SemaphoreType.DMA,
        ],
        compiler_params=pltpu.CompilerParams(collective_id=1, has_side_effects=True),
        name="exchange",
    )(outgoing)


def collect_kernel(idx_ref, rec_ref, out_ref, tab, stage):
    src = iota((LANES, 2 * LANES), 0)
    dst = iota((LANES, 2 * LANES), 1)
    half = dst // LANES
    lane2 = dst - half * LANES
    total = NB * CAP_ROWS
    for pair in range(GROUPS // 2):
        spread = one_hot(
            jnp.logical_and(
                lane2 < SLOT_GROUPS * CB, src == (2 * pair + half) * CB + lane2 - (lane2 // CB) * CB
            )
        )

        def fill(i, _, spread=spread, pair=pair):
            both = mm(rec_ref[i], spread)
            a = pl.multiple_of(i * CAP_ROWS, CAP_ROWS)
            tab[pl.ds(2 * pair * total + a, CAP_ROWS), :] = both[:, :LANES]
            tab[pl.ds((2 * pair + 1) * total + a, CAP_ROWS), :] = both[:, LANES:]
            return 0

        lax.fori_loop(0, NB, fill, 0)

    lane = iota((1, LANES), 1)
    unroll = 8

    def block(q, _):
        for u in range(unroll):
            r = q * unroll + u
            acc = tab[pl.ds(idx_ref[r], 1), :]
            for g in range(1, SLOT_GROUPS):
                acc = jnp.where(lane >= CB * g, tab[pl.ds(idx_ref[g * SLOT_ROWS + r], 1), :], acc)
            stage[pl.ds(r, 1), :] = acc
        return 0

    lax.fori_loop(0, SLOT_ROWS // unroll, block, 0)
    s_row = iota((SLOT_GROUPS * 16, LANES), 0)
    s_lane = iota((SLOT_GROUPS * 16, LANES), 1)
    group = s_row // 16
    comp = s_row - group * 16
    turn = one_hot(jnp.logical_and(comp < CB, s_lane == group * CB + comp))
    width = out_ref.shape[1]
    turned = lax.dot_general(
        turn, stage[...].astype(BF16), (((1,), (1,)), ((), ())), preferred_element_type=F32
    )
    for g in range(SLOT_GROUPS):
        size = min(SLOT_ROWS, width - g * SLOT_ROWS)
        out_ref[:, g * SLOT_ROWS : g * SLOT_ROWS + size] = turned[16 * g : 16 * g + CB, :size].astype(BF16)


def collect(idx, received, width):
    smem = pl.BlockSpec(memory_space=pltpu.SMEM)
    vmem = pl.BlockSpec(memory_space=pltpu.VMEM)
    return pl.pallas_call(
        collect_kernel,
        out_shape=jax.ShapeDtypeStruct((CB, width), BF16),
        in_specs=[smem, vmem],
        out_specs=vmem,
        scratch_shapes=[
            pltpu.VMEM((GROUPS * NB * CAP_ROWS, LANES), F32), pltpu.VMEM((SLOT_ROWS, LANES), F32),
        ],
        compiler_params=pltpu.CompilerParams(vmem_limit_bytes=40 << 20),
        name="collect",
    )(idx, received)


def coefficients(comp_here, pts_here):
    grid_rows = ROWS * NB
    lane = jnp.arange(LANES, dtype=jnp.int32)
    rr = lane // CB
    comp = comp_here * CB + lane % CB
    quad = comp_here % 4
    north = quad < 2
    band_row = jnp.where(north, rr - ITERS, ROWS - 1 + ITERS - rr)
    row = (pts_here * ROWS + band_row).astype(F32)

    def cosines(row_ids):
        radians = (45.0 + 0.1 * (row_ids + 0.5 - 0.5 * grid_rows)) * (math.pi / 180.0)
        return jnp.cos(radians), jnp.cos(radians + 0.05 * math.pi / 180.0)

    cos_mid, cos_upper = cosines(row)
    cos_lower = cosines(row - 1.0)[1]
    freq = (comp // ND).astype(F32)
    angle = ((comp % ND).astype(F32) + 0.5) * (2.0 * math.pi / ND)
    top = math.cos((45.0 + 0.05 * grid_rows) * math.pi / 180.0)
    speed = 0.6 * top * jnp.power(jnp.float32(1.1), -freq)
    east_x = jnp.abs(speed * jnp.cos(angle))
    north_y = jnp.abs(speed * jnp.sin(angle))
    ax = east_x / cos_mid
    up = north_y * jnp.where(north, cos_lower, cos_upper) / cos_mid
    dn = north_y * jnp.where(north, cos_upper, cos_lower) / cos_mid
    live = rr < ROWS + ITERS
    rows = [jnp.where(live, value, 0.0) for value in (ax, up, dn)]
    return jnp.stack(rows + [jnp.zeros((LANES,), F32)] * 5)


def local(spectra, land_mask, send_rows, row_counts, return_index):
    comp_here = lax.axis_index("comp")
    pts_here = lax.axis_index("pts")
    north = comp_here % 4 < 2

    cells = send_rows[0]
    row = cells // LON
    cell_row = jnp.where(north, row, ROWS - 1 - row) * LON + cells - row * LON
    cell_idx = jnp.pad(cell_row, ((0, 0), (0, CAP_ROWS * GROUPS - CAP))).reshape(-1)
    counts_out = lax.dynamic_slice_in_dim(row_counts, pts_here, 1, 0)[0]
    blocks = (counts_out + 2 * GROUPS - 1) // (2 * GROUPS)

    counts_in = lax.dynamic_slice_in_dim(row_counts, pts_here, 1, 1)[:, 0]
    offsets = jnp.cumsum(counts_in) - counts_in
    picked = return_index[0]
    source = jnp.sum((picked[:, None] >= offsets[None, :]).astype(jnp.int32), axis=1) - 1
    start = jnp.sum(
        jnp.where(source[:, None] == jnp.arange(NB, dtype=jnp.int32)[None, :], offsets[None, :], 0), axis=1
    )
    within = picked - start
    slot_row = within // GROUPS
    slot = (within - slot_row * GROUPS) * (NB * CAP_ROWS) + source * CAP_ROWS + slot_row
    slot_idx = jnp.pad(slot, (0, SLOT_ROWS * SLOT_GROUPS - slot.shape[0]))

    values = propagate(spectra, land_mask, coefficients(comp_here, pts_here))
    outgoing = select_cells(blocks, cell_idx, values)
    received = exchange(outgoing)
    return collect(slot_idx, received, picked.shape[0])


def solution(mesh):
    placed = (P("comp", "pts"), P("pts", None), P("pts", None, None), P(), P("pts", None))
    return jax.shard_map(
        local, mesh=mesh, in_specs=placed, out_specs=P("comp", "pts"), check_vma=False
    )
```

time: 235 us -> 113 us (0.48)
  the two profiles are of different devices: /device:TPU:32 before, /device:TPU:8 now
where the time goes in v1:
time: 113 us; the launch traced here: 112 us
  Pallas kernels  108 us (96%)
  local copies, waits for them, and re-layouts  3.52 us (3%)
  other arithmetic  1.2 us (1%)
    pallas_call x1, Pallas kernels, propagate(): pl.pallas_call(propagate_kernel, out_shape=jax.ShapeDtypeStruct((LON, LAN...  33.2 us
    pallas_call x1, Pallas kernels, collect(): pl.pallas_call(collect_kernel, out_shape=jax.ShapeDtypeStruct((CB, width)...  29.5 us
    pallas_call x1, Pallas kernels, select_cells(): pl.pallas_call(select_kernel, out_shape=jax.ShapeDtypeStruct((NB, CAP_ROW...  28.9 us
    pallas_call x1, Pallas kernels, exchange(): pl.pallas_call(exchange_kernel, out_shape=jax.ShapeDtypeStruct(outgoing.s...  15.9 us
    unnamed x14, local copies, waits for them, and re-layouts  3.31 us

profile of v1, /device:TPU:8, one launch (start us, length us, event | category | flops | bytes accessed | tf_op | source)
XLA Modules:
  0.0 112.4 jit_solution(14636914415069212411)
XLA Ops:
  0.0 0.1 divide_select_fusion
  0.1 0.1 fusion.18
  0.2 0.0 copy-start.2
  0.2 1.0 copy-done.2
  1.3 0.0 copy-start.3
  1.3 0.9 copy-done.3
  2.2 0.0 copy-start.4
  2.2 33.2 %propagate.1.v_ref = bf16[3600,128]{1,0:T(8,128)(2,1)S(1)} custom-call(bf16[225,1152]{1,0:T(8,128)(2,1)S(1)} %copy-done.2, s32[8,3600]{1,0:T(8,128)S(1)} %copy-done.3, f32[8,128]{1,0:T(8,128)S(1)} %stack.10.coef_ref), custom_call_target="tpu_custom_call" | custom-call | tf_op jit(solution)/shard_map/propagate/pallas_call | solution.py:213
  35.4 0.0 copy-done.4
  35.4 0.1 fusion.2
  35.5 0.0 copy-start.6
  35.5 0.1 reshape.261.idx_ref
  35.6 0.6 copy-done.6
  36.2 28.9 %select_cells.1.src_ref = bf16[16,96,128]{2,1,0:T(8,128)(2,1)S(1)} custom-call(s32[16]{0:T(128)S(1)} %bitcast_select_fusion.rows_ref, s32[21504]{0:T(1024)S(1)} %reshape.261.idx_ref, bf16[3600,128]{1,0:T(8,128)(2,1)S(1)} %propagate.1.v_ref), custom_call_target="tpu_custom_call" | custom-call | tf_op jit(solution)/shard_map/select_cells/pallas_call | solution.py:289
  65.1 0.0 copy-start.1
  65.1 0.7 copy-done.1
  65.9 0.0 copy-start.5
  65.9 15.9 %exchange.1.rec_ref = bf16[16,96,128]{2,1,0:T(8,128)(2,1)} custom-call(bf16[16,96,128]{2,1,0:T(8,128)(2,1)} %copy-done.1), custom_call_target="tpu_custom_call" | custom-call | tf_op jit(solution)/shard_map/exchange/pallas_call | solution.py:327
  81.8 0.1 constant_dynamic-slice_fusion
  81.9 0.0 copy-start
  81.9 0.2 subtract_reduce_fusion
  82.1 0.0 copy-done.5
  82.1 0.1 reduce
  82.3 0.3 convert_reduce_fusion
  82.5 0.2 select_reduce_fusion
  82.8 0.1 add_add_fusion
  82.9 0.0 copy-done
  82.9 29.5 %collect.1 = bf16[9,13120]{1,0:T(8,128)(2,1)} custom-call(s32[13312]{0:T(1024)S(1)} %pad.8.idx_ref, bf16[16,96,128]{2,1,0:T(8,128)(2,1)S(1)} %copy-done), custom_call_target="tpu_custom_call" | custom-call | tf_op jit(solution)/shard_map/collect/pallas_call | solution.py:392
  (8 shorter events, 0.1 us)
Async XLA Ops:
  0.2 1.0 copy-start.2
  1.3 0.9 copy-start.3
  2.2 33.2 %copy-start.4 = (s32[1,16,1280]{2,1,0:T(8,128)S(1)}, s32[1,16,1280]{2,1,0:T(8,128)}, u32[]{:S(2)}) copy-start(s32[1,16,1280]{2,1,0:T(8,128)} %param.7) | copy-start | bytes 245764
  35.5 0.7 copy-start.6
  65.1 0.7 copy-start.1
  65.9 16.3 %copy-start.5 = (s32[1,13120]{1,0:T(1,128)S(1)}, s32[1,13120]{1,0:T(1,128)}, u32[]{:S(2)}) copy-start(s32[1,13120]{1,0:T(1,128)} %param.9) | copy-start | bytes 157444
  81.9 1.0 copy-start

commit v2 on v1

--- a/solution.py
+++ b/solution.py
@@ -243,7 +243,6 @@
     dst = iota((LANES, 2 * LANES), 1)
     half = dst // LANES
     lane2 = dst - half * LANES
-    chunk = 240
     for pair in range(ROWS // 2):
         spread = one_hot(
             jnp.logical_and(
@@ -251,14 +250,9 @@
             )
         )
 
-        def fill(i, _, spread=spread, pair=pair):
-            a = pl.multiple_of(i * chunk, chunk)
-            both = mm(v_ref[pl.ds(a, chunk), :], spread)
-            tab[pl.ds(2 * pair * LON + a, chunk), :] = both[:, :LANES]
-            tab[pl.ds((2 * pair + 1) * LON + a, chunk), :] = both[:, LANES:]
-            return 0
-
-        lax.fori_loop(0, LON // chunk, fill, 0)
+        both = mm(v_ref[...], spread)
+        tab[2 * pair * LON : (2 * pair + 1) * LON, :] = both[:, :LANES]
+        tab[(2 * pair + 1) * LON : (2 * pair + 2) * LON, :] = both[:, LANES:]
 
     lane = iota((1, LANES), 1)
     unroll = 2
@@ -270,9 +264,10 @@
             for u in range(unroll):
                 r = q * unroll + u
                 e = base + r * GROUPS
-                acc = tab[pl.ds(idx_ref[e], 1), :]
+                at = idx_ref.at[pl.ds(e, GROUPS)]
+                acc = tab[pl.ds(at[0], 1), :]
                 for g in range(1, GROUPS):
-                    acc = jnp.where(lane >= CB * g, tab[pl.ds(idx_ref[e + g], 1), :], acc)
+                    acc = jnp.where(lane >= CB * g, tab[pl.ds(at[g], 1), :], acc)
                 stage[pl.ds(r, 1), :] = acc
             return 0
 
@@ -350,14 +345,9 @@
             )
         )
 
-        def fill(i, _, spread=spread, pair=pair):
-            both = mm(rec_ref[i], spread)
-            a = pl.multiple_of(i * CAP_ROWS, CAP_ROWS)
-            tab[pl.ds(2 * pair * total + a, CAP_ROWS), :] = both[:, :LANES]
-            tab[pl.ds((2 * pair + 1) * total + a, CAP_ROWS), :] = both[:, LANES:]
-            return 0
-
-        lax.fori_loop(0, NB, fill, 0)
+        both = mm(rec_ref[...].reshape(total, LANES), spread)
+        tab[2 * pair * total : (2 * pair + 1) * total, :] = both[:, :LANES]
+        tab[(2 * pair + 1) * total : (2 * pair + 2) * total, :] = both[:, LANES:]
 
     lane = iota((1, LANES), 1)
     unroll = 8

time: 113 us -> 87.4 us (0.77)
  the two profiles are of different devices: /device:TPU:8 before, /device:TPU:32 now
where the time goes in v2:
time: 87.4 us; the launch traced here: 85.8 us
  Pallas kernels  81 us (93%)
  local copies, waits for them, and re-layouts  3.52 us (4%)
  other arithmetic  1.2 us (1%)
    pallas_call x1, Pallas kernels, propagate(): pl.pallas_call(propagate_kernel, out_shape=jax.ShapeDtypeStruct((LON, LAN...  33 us
    pallas_call x1, Pallas kernels, exchange(): pl.pallas_call(exchange_kernel, out_shape=jax.ShapeDtypeStruct(outgoing.s...  19.7 us
    pallas_call x1, Pallas kernels, collect(): pl.pallas_call(collect_kernel, out_shape=jax.ShapeDtypeStruct((CB, width)...  15.3 us
    pallas_call x1, Pallas kernels, select_cells(): pl.pallas_call(select_kernel, out_shape=jax.ShapeDtypeStruct((NB, CAP_ROW...  12.9 us
    unnamed x14, local copies, waits for them, and re-layouts  3.31 us

profile of v2, /device:TPU:32, one launch (start us, length us, event | category | flops | bytes accessed | tf_op | source)
XLA Modules:
  0.0 85.8 jit_solution(17326899496114499714)
XLA Ops:
  0.0 0.1 divide_select_fusion
  0.1 0.1 fusion.18
  0.2 0.0 copy-start.2
  0.2 1.0 %copy-done.2 = bf16[225,1152]{1,0:T(8,128)(2,1)S(1)} copy-done((bf16[225,1152]{1,0:T(8,128)(2,1)S(1)}, bf16[225,1152]{1,0:T(8,128)(2,1)}, u32[]{:S(2)}) %copy-start.2) | copy-done | bytes 518424
  1.3 0.0 copy-start.3
  1.3 0.9 %copy-done.3 = s32[8,3600]{1,0:T(8,128)S(1)} copy-done((s32[8,3600]{1,0:T(8,128)S(1)}, s32[8,3600]{1,0:T(8,128)}, u32[]{:S(2)}) %copy-start.3) | copy-done | bytes 115224
  2.2 0.0 copy-start.4
  2.2 33.0 %propagate.1.v_ref = bf16[3600,128]{1,0:T(8,128)(2,1)S(1)} custom-call(bf16[225,1152]{1,0:T(8,128)(2,1)S(1)} %copy-done.2, s32[8,3600]{1,0:T(8,128)S(1)} %copy-done.3, f32[8,128]{1,0:T(8,128)S(1)} %stack.10.coef_ref), custom_call_target="tpu_custom_call" | custom-call | tf_op jit(solution)/shard_map/propagate/pallas_call | solution.py:213
  35.2 0.0 copy-done.4
  35.2 0.1 fusion.2
  35.3 0.0 copy-start.6
  35.3 0.1 reshape.261.idx_ref
  35.4 0.6 copy-done.6
  36.1 12.9 %select_cells.1.src_ref = bf16[16,96,128]{2,1,0:T(8,128)(2,1)S(1)} custom-call(s32[16]{0:T(128)S(1)} %bitcast_select_fusion.rows_ref, s32[21504]{0:T(1024)S(1)} %reshape.261.idx_ref, bf16[3600,128]{1,0:T(8,128)(2,1)S(1)} %propagate.1.v_ref), custom_call_target="tpu_custom_call" | custom-call | tf_op jit(solution)/shard_map/select_cells/pallas_call | solution.py:284
  49.0 0.0 copy-start.1
  49.0 0.7 copy-done.1
  49.7 0.0 copy-start.5
  49.7 19.7 %exchange.1.rec_ref = bf16[16,96,128]{2,1,0:T(8,128)(2,1)} custom-call(bf16[16,96,128]{2,1,0:T(8,128)(2,1)} %copy-done.1), custom_call_target="tpu_custom_call" | custom-call | tf_op jit(solution)/shard_map/exchange/pallas_call | solution.py:322
  69.4 0.1 constant_dynamic-slice_fusion
  69.5 0.0 copy-start
  69.5 0.2 subtract_reduce_fusion
  69.7 0.0 copy-done.5
  69.7 0.1 reduce
  69.9 0.3 convert_reduce_fusion
  70.1 0.2 select_reduce_fusion
  70.4 0.1 add_add_fusion
  70.5 0.0 copy-done
  70.5 15.3 %collect.1 = bf16[9,13120]{1,0:T(8,128)(2,1)} custom-call(s32[13312]{0:T(1024)S(1)} %pad.8.idx_ref, bf16[16,96,128]{2,1,0:T(8,128)(2,1)S(1)} %copy-done), custom_call_target="tpu_custom_call" | custom-call | tf_op jit(solution)/shard_map/collect/pallas_call | solution.py:382
  (8 shorter events, 0.1 us)
Async XLA Ops:
  0.2 1.0 %copy-start.2 = (bf16[225,1152]{1,0:T(8,128)(2,1)S(1)}, bf16[225,1152]{1,0:T(8,128)(2,1)}, u32[]{:S(2)}) copy-start(bf16[225,1152]{1,0:T(8,128)(2,1)} %x_ref.1) | copy-start | bytes 1555204
  1.3 0.9 %copy-start.3 = (s32[8,3600]{1,0:T(8,128)S(1)}, s32[8,3600]{1,0:T(8,128)}, u32[]{:S(2)}) copy-start(s32[8,3600]{1,0:T(8,128)} %mask_ref.1) | copy-start | bytes 345604
  2.2 33.0 %copy-start.4 = (s32[1,16,1280]{2,1,0:T(8,128)S(1)}, s32[1,16,1280]{2,1,0:T(8,128)}, u32[]{:S(2)}) copy-start(s32[1,16,1280]{2,1,0:T(8,128)} %param.7) | copy-start | bytes 245764
  35.3 0.7 copy-start.6
  49.0 0.7 copy-start.1
  49.7 20.0 %copy-start.5 = (s32[1,13120]{1,0:T(1,128)S(1)}, s32[1,13120]{1,0:T(1,128)}, u32[]{:S(2)}) copy-start(s32[1,13120]{1,0:T(1,128)} %param.9) | copy-start | bytes 157444
  69.5 1.0 %copy-start = (bf16[16,96,128]{2,1,0:T(8,128)(2,1)S(1)}, bf16[16,96,128]{2,1,0:T(8,128)(2,1)}, u32[]{:S(2)}) copy-start(bf16[16,96,128]{2,1,0:T(8,128)(2,1)} %exchange.1.rec_ref) | copy-start | bytes 1179652

commit v3 on v2

v3 whole, which is shorter than its diff:
```python
import functools
import math

import jax
import jax.numpy as jnp
from jax import lax
from jax.experimental import pallas as pl
from jax.experimental.pallas import tpu as pltpu
from jax.sharding import PartitionSpec as P

ND = 36
ITERS = 4
LANES = 128
CB = 9
ROWS = 8
OWN = ITERS * CB
LON = 3600
LB = 225
SEG = 80
NB = 16
PAD = 8
GROUPS = 14
CAP = 1280
CAP_ROWS = 96
USED_ROWS = 92
SLOT_ROWS = 1024
SLOT_GROUPS = 13
F32 = jnp.float32
BF16 = jnp.bfloat16


def iota(shape, dim):
    return lax.broadcasted_iota(jnp.int32, shape, dim)


def one_hot(cond):
    return jnp.where(cond, 1.0, 0.0).astype(BF16)


def mm(a, b):
    return jnp.dot(a, b, preferred_element_type=F32)


def send(src, dst, send_sem, recv_sem, **where):
    return pltpu.make_async_remote_copy(
        src_ref=src, dst_ref=dst, send_sem=send_sem, recv_sem=recv_sem,
        device_id=where, device_id_type=pl.DeviceIdType.MESH,
    )


def merge_rows(tab, at, groups, stride, lane):
    row = tab[pl.ds(at[0], 1), :]
    for g in range(1, groups):
        row = jnp.where(lane >= CB * g, tab[pl.ds(at[g * stride], 1), :], row)
    return row


def spread_matrix(first, live):
    src = iota((LANES, 2 * LANES), 0)
    dst = iota((LANES, 2 * LANES), 1)
    half = dst // LANES
    lane2 = dst - half * LANES
    return one_hot(
        jnp.logical_and(lane2 < live * CB, src == first + half * CB + lane2 - (lane2 // CB) * CB)
    )


def partners(c):
    z = c // 2
    order = []
    for dist in (4, 3, 2, 1):
        for chip in ((4,) if dist == 4 else (dist, 8 - dist)):
            for core in range(2):
                order.append(lax.rem(z + chip, 8) * 2 + core)
    order.append(z * 2 + 1 - (c - z * 2))
    return order


def whole_kernel(
    x_ref, mask_ref, coef_ref, cell_ref, slot_ref, out_ref,
    sendbuf, piece, hsend, hrecv, ymid, mprev, mown, mnext, mstack, mexp, mdown, kbuf, va, vb,
    vfin, tab, stage, outgo, income, cells, slots,
    s_send, s_recv, h_send, h_recv, m_send, m_recv, l_sem, o_send, o_recv,
):
    c = lax.axis_index("comp")
    j = lax.axis_index("pts")
    nxt = lax.rem(j + 1, NB)
    prv = lax.rem(j + NB - 1, NB)
    quad = lax.rem(c, 4)
    north = quad < 2
    east = jnp.logical_or(quad == 0, quad == 3)
    down = jnp.where(north, nxt, prv)
    others = partners(c)

    barrier = pltpu.get_barrier_semaphore()
    for s in range(1, NB):
        pl.semaphore_signal(
            barrier, inc=1, device_id={"comp": lax.rem(c + s, NB)}, device_id_type=pl.DeviceIdType.MESH
        )
        pl.semaphore_signal(
            barrier, inc=1, device_id={"pts": lax.rem(j + s, NB)}, device_id_type=pl.DeviceIdType.MESH
        )
    get_mask = pltpu.make_async_copy(mask_ref, mown, l_sem.at[1])
    get_cells = pltpu.make_async_copy(cell_ref, cells, l_sem.at[2])
    get_slots = pltpu.make_async_copy(slot_ref, slots, l_sem.at[3])
    get_mask.start()
    get_cells.start()
    get_slots.start()

    ymid[LB : 3 * SEG, :] = jnp.zeros((3 * SEG - LB, LANES), F32)
    m_id = iota((ROWS * NB * CB, LANES), 0)
    lane = iota((1, LANES), 1)
    pos = lane // CB
    lane_s = iota((SEG, LANES), 1)
    x = x_ref[...]
    for t in range(NB):
        row = pos if t % 4 < 2 else ROWS - 1 - pos
        want = jnp.where(lane < ROWS * CB, row * (NB * CB) + t * CB + lane - pos * CB, -1)
        ymid[0:LB, :] = mm(x, one_hot(m_id == want))
        y0 = ymid[0:SEG, :]
        y1 = pltpu.roll(ymid[SEG : 2 * SEG, :], 72, 1)
        y2 = pltpu.roll(ymid[2 * SEG : 3 * SEG, :], 16, 1)
        sendbuf[t, :, 0:LANES] = jnp.where(lane_s < 72, y0, y1).astype(BF16)
        sendbuf[t, :, LANES : 2 * LANES] = jnp.where(lane_s < 16, y1, y2).astype(BF16)

    get_mask.wait()
    pl.semaphore_wait(barrier, 2 * (NB - 1))

    copies = []
    for to in others:
        copies.append(send(sendbuf.at[to], piece.at[c], s_send.at[to], s_recv.at[c], comp=to))
        copies[-1].start()
    m_up = send(mown, mprev, m_send.at[0], m_recv.at[0], pts=nxt)
    m_up.start()
    m_dn = send(mown, mnext, m_send.at[1], m_recv.at[1], pts=prv)
    m_dn.start()
    own = pltpu.make_async_copy(sendbuf.at[c], piece.at[c], l_sem.at[0])
    own.start()

    m_up.wait()
    m_dn.wait()
    mstack[0:ROWS, :] = jnp.where(j > 0, mprev[...], 0).astype(F32)
    mstack[ROWS : 2 * ROWS, :] = mown[...].astype(F32)
    mstack[2 * ROWS : 3 * ROWS, :] = jnp.where(j < NB - 1, mnext[...], 0).astype(F32)
    g_id = iota((3 * ROWS, LANES), 0)
    l_id = iota((3 * ROWS, LANES), 1)
    rr = l_id // CB
    live = rr < ROWS + ITERS
    e_here = one_hot(jnp.logical_and(live, g_id == jnp.where(north, rr + 4, 19 - rr)))
    e_down = one_hot(jnp.logical_and(live, g_id == jnp.where(north, rr + 5, 18 - rr)))
    e_both = jnp.concatenate([e_here, e_down], axis=1)
    stack = mstack[...].astype(BF16)
    both = lax.dot_general(stack, e_both, (((0,), (0,)), ((), ())), preferred_element_type=F32)
    mexp[PAD : PAD + LON, :] = both[:, :LANES]
    mdown[...] = both[:, LANES:]
    mexp[PAD - 1 : PAD, :] = mexp[PAD + LON - 1 : PAD + LON, :]
    mexp[PAD + LON : PAD + LON + 1, :] = mexp[PAD : PAD + 1, :]
    ax = coef_ref[0:1, :]
    ay = coef_ref[1:2, :]
    ad = coef_ref[2:3, :]
    step_rows = 120
    for i in range(LON // step_rows):
        a = PAD + i * step_rows
        m = mexp[a : a + step_rows, :]
        lon_down = jnp.where(
            east, mexp[a + 1 : a + 1 + step_rows, :], mexp[a - 1 : a - 1 + step_rows, :]
        )
        kbuf[i * step_rows : (i + 1) * step_rows, :] = m * (
            1.0 - ax * lon_down - ad * mdown[i * step_rows : (i + 1) * step_rows, :]
        )

    src = iota((2 * LANES, LANES), 0)
    dst = iota((2 * LANES, LANES), 1)
    seg = dst // OWN
    h_pack = one_hot(
        jnp.logical_and(seg < 3, src == seg * (ROWS * CB) + (ROWS - ITERS) * CB + dst - seg * OWN)
    )
    hops = []
    for b in [c] + others:
        if not hops:
            own.wait()
        else:
            send(sendbuf.at[b], piece.at[b], s_send.at[b], s_recv.at[b], comp=b).wait_recv()
        hsend[b] = mm(piece[b], h_pack).astype(BF16)
        hops.append(send(hsend.at[b], hrecv.at[b], h_send.at[b], h_recv.at[b], pts=down))
        hops[-1].start()

    u_src = iota((2 * LANES, 3 * LANES), 0)
    u_dst = iota((2 * LANES, 3 * LANES), 1)
    u_seg = u_dst // LANES
    u_lane = u_dst - u_seg * LANES
    own_lane = jnp.logical_and(u_lane >= OWN, u_lane < OWN + ROWS * CB)
    unpack = one_hot(jnp.logical_and(own_lane, u_src == u_seg * (ROWS * CB) + u_lane - OWN))
    hu_src = iota((LANES, 3 * LANES), 0)
    hu_dst = iota((LANES, 3 * LANES), 1)
    hu_seg = hu_dst // LANES
    hu_lane = hu_dst - hu_seg * LANES
    h_unpack = one_hot(jnp.logical_and(hu_lane < OWN, hu_src == hu_seg * OWN + hu_lane))
    for hop in hops:
        hop.wait_recv()
    for b in range(NB):
        full = mm(piece[b], unpack) + mm(hrecv[b], h_unpack)
        for t in range(3):
            size = min(SEG, LB - t * SEG)
            a = PAD + b * LB + t * SEG
            va[a : a + size, :] = full[:size, t * LANES : (t + 1) * LANES] * mexp[a : a + size, :]

    for it in range(ITERS):
        v, w = (va, vb) if it % 2 == 0 else (vb, va)
        v[PAD - 1 : PAD, :] = v[PAD + LON - 1 : PAD + LON, :]
        v[PAD + LON : PAD + LON + 1, :] = v[PAD : PAD + 1, :]
        for i in range(LON // step_rows):
            a = PAD + i * step_rows
            k = i * step_rows
            here = v[a : a + step_rows, :]
            side = jnp.where(east, v[a - 1 : a - 1 + step_rows, :], v[a + 1 : a + 1 + step_rows, :])
            new = kbuf[k : k + step_rows, :] * here + mexp[a : a + step_rows, :] * (
                ax * side + ay * pltpu.roll(here, CB, 1)
            )
            if it < ITERS - 1:
                w[a : a + step_rows, :] = new
            else:
                vfin[k : k + step_rows, :] = new.astype(BF16)

    for pair in range(ROWS // 2):
        both = mm(vfin[...], spread_matrix(OWN + 2 * pair * CB, GROUPS))
        tab[2 * pair * LON : (2 * pair + 1) * LON, :] = both[:, :LANES]
        tab[(2 * pair + 1) * LON : (2 * pair + 2) * LON, :] = both[:, LANES:]
    get_cells.wait()
    unroll = 23

    def fill_block(d):
        def rows(q, _):
            for u in range(unroll):
                r = q * unroll + u
                at = cells.at[pl.ds(d * (USED_ROWS * GROUPS) + r, (GROUPS - 1) * USED_ROWS + 1)]
                stage[pl.ds(r, 1), :] = merge_rows(tab, at, GROUPS, USED_ROWS, lane)
            return 0

        lax.fori_loop(0, USED_ROWS // unroll, rows, 0)

    stage[USED_ROWS:CAP_ROWS, :] = jnp.zeros((CAP_ROWS - USED_ROWS, LANES), F32)

    def owner(s, _):
        d = lax.rem(j + s, NB)
        fill_block(d)
        outgo[d] = stage[0:CAP_ROWS, :].astype(BF16)
        send(outgo.at[d], income.at[j], o_send.at[d], o_recv.at[j], pts=d).start()
        return 0

    lax.fori_loop(1, NB, owner, 0)
    fill_block(j)
    income[j] = stage[0:CAP_ROWS, :].astype(BF16)

    def arrive(s, _):
        d = lax.rem(j + s, NB)
        copy = send(outgo.at[d], income.at[d], o_send.at[d], o_recv.at[d], pts=d)
        copy.wait_send()
        copy.wait_recv()
        return 0

    lax.fori_loop(1, NB, arrive, 0)

    total = NB * CAP_ROWS
    got = income[...].reshape(total, LANES)
    for pair in range(GROUPS // 2):
        both = mm(got, spread_matrix(2 * pair * CB, SLOT_GROUPS))
        tab[2 * pair * total : (2 * pair + 1) * total, :] = both[:, :LANES]
        tab[(2 * pair + 1) * total : (2 * pair + 2) * total, :] = both[:, LANES:]
    get_slots.wait()
    slot_unroll = 16

    def slot_rows(q, _):
        for u in range(slot_unroll):
            r = q * slot_unroll + u
            at = slots.at[pl.ds(r, (SLOT_GROUPS - 1) * SLOT_ROWS + 1)]
            stage[pl.ds(r, 1), :] = merge_rows(tab, at, SLOT_GROUPS, SLOT_ROWS, lane)
        return 0

    lax.fori_loop(0, SLOT_ROWS // slot_unroll, slot_rows, 0)
    t_row = iota((SLOT_GROUPS * 16, LANES), 0)
    t_lane = iota((SLOT_GROUPS * 16, LANES), 1)
    group = t_row // 16
    comp = t_row - group * 16
    turn = one_hot(jnp.logical_and(comp < CB, t_lane == group * CB + comp))
    width = out_ref.shape[1]
    turned = lax.dot_general(
        turn, stage[...].astype(BF16), (((1,), (1,)), ((), ())), preferred_element_type=F32
    )
    for g in range(SLOT_GROUPS):
        size = min(SLOT_ROWS, width - g * SLOT_ROWS)
        out_ref[:, g * SLOT_ROWS : g * SLOT_ROWS + size] = turned[16 * g : 16 * g + CB, :size].astype(BF16)

    for copy in copies:
        copy.wait_send()
    for hop in hops:
        hop.wait_send()


def whole(x, mask, coef, cell_idx, slot_idx, width):
    dma = pltpu.SemaphoreType.DMA
    vmem = pl.BlockSpec(memory_space=pltpu.VMEM)
    hbm = pl.BlockSpec(memory_space=pltpu.HBM)
    wrapped = PAD + LON + 8
    return pl.pallas_call(
        whole_kernel,
        out_shape=jax.ShapeDtypeStruct((CB, width), BF16),
        in_specs=[vmem, hbm, vmem, hbm, hbm],
        out_specs=vmem,
        scratch_shapes=[
            pltpu.VMEM((NB, SEG, 2 * LANES), BF16),
            pltpu.VMEM((NB, SEG, 2 * LANES), BF16),
            pltpu.VMEM((NB, SEG, LANES), BF16),
            pltpu.VMEM((NB, SEG, LANES), BF16),
            pltpu.VMEM((3 * SEG, LANES), F32),
            pltpu.VMEM((ROWS, LON), jnp.int32),
            pltpu.VMEM((ROWS, LON), jnp.int32),
            pltpu.VMEM((ROWS, LON), jnp.int32),
            pltpu.VMEM((3 * ROWS, LON), F32),
            pltpu.VMEM((wrapped, LANES), F32),
            pltpu.VMEM((LON, LANES), F32),
            pltpu.VMEM((LON, LANES), F32),
            pltpu.VMEM((wrapped, LANES), F32),
            pltpu.VMEM((wrapped, LANES), F32),
            pltpu.VMEM((LON, LANES), BF16),
            pltpu.VMEM((ROWS * LON, LANES), F32),
            pltpu.VMEM((SLOT_ROWS, LANES), F32),
            pltpu.VMEM((NB, CAP_ROWS, LANES), BF16),
            pltpu.VMEM((NB, CAP_ROWS, LANES), BF16),
            pltpu.SMEM(cell_idx.shape, jnp.int32),
            pltpu.SMEM(slot_idx.shape, jnp.int32),
            dma((NB,)), dma((NB,)), dma((NB,)), dma((NB,)), dma((2,)), dma((2,)), dma((4,)),
            dma((NB,)), dma((NB,)),
        ],
        compiler_params=pltpu.CompilerParams(
            collective_id=0, has_side_effects=True, vmem_limit_bytes=52 << 20
        ),
        name="propagate_and_return",
    )(x, mask, coef, cell_idx, slot_idx)


def coefficients(comp_here, pts_here):
    grid_rows = ROWS * NB
    lane = jnp.arange(LANES, dtype=jnp.int32)
    rr = lane // CB
    comp = comp_here * CB + lane % CB
    quad = comp_here % 4
    north = quad < 2
    band_row = jnp.where(north, rr - ITERS, ROWS - 1 + ITERS - rr)
    row = (pts_here * ROWS + band_row).astype(F32)

    def cosines(row_ids):
        radians = (45.0 + 0.1 * (row_ids + 0.5 - 0.5 * grid_rows)) * (math.pi / 180.0)
        return jnp.cos(radians), jnp.cos(radians + 0.05 * math.pi / 180.0)

    cos_mid, cos_upper = cosines(row)
    cos_lower = cosines(row - 1.0)[1]
    freq = (comp // ND).astype(F32)
    angle = ((comp % ND).astype(F32) + 0.5) * (2.0 * math.pi / ND)
    top = math.cos((45.0 + 0.05 * grid_rows) * math.pi / 180.0)
    speed = 0.6 * top * jnp.power(jnp.float32(1.1), -freq)
    east_x = jnp.abs(speed * jnp.cos(angle))
    north_y = jnp.abs(speed * jnp.sin(angle))
    ax = east_x / cos_mid
    up = north_y * jnp.where(north, cos_lower, cos_upper) / cos_mid
    dn = north_y * jnp.where(north, cos_upper, cos_lower) / cos_mid
    live = rr < ROWS + ITERS
    rows = [jnp.where(live, value, 0.0) for value in (ax, up, dn)]
    return jnp.stack(rows + [jnp.zeros((LANES,), F32)] * 5)


def local(spectra, land_mask, send_rows, row_counts, return_index):
    comp_here = lax.axis_index("comp")
    pts_here = lax.axis_index("pts")
    north = comp_here % 4 < 2

    cells = send_rows[0]
    row = cells // LON
    cell_row = jnp.where(north, row, ROWS - 1 - row) * LON + cells - row * LON
    cell_idx = jnp.pad(cell_row, ((0, 0), (0, USED_ROWS * GROUPS - CAP))).reshape(-1)

    counts_in = lax.dynamic_slice_in_dim(row_counts, pts_here, 1, 1)[:, 0]
    offsets = jnp.cumsum(counts_in) - counts_in
    picked = return_index[0]
    source = jnp.sum((picked[:, None] >= offsets[None, :]).astype(jnp.int32), axis=1) - 1
    start = jnp.sum(
        jnp.where(source[:, None] == jnp.arange(NB, dtype=jnp.int32)[None, :], offsets[None, :], 0), axis=1
    )
    within = picked - start
    group = within // USED_ROWS
    slot = group * (NB * CAP_ROWS) + source * CAP_ROWS + within - group * USED_ROWS
    slot_idx = jnp.pad(slot, (0, SLOT_ROWS * SLOT_GROUPS - slot.shape[0]))
    coef = coefficients(comp_here, pts_here)
    return whole(spectra, land_mask, coef, cell_idx, slot_idx, picked.shape[0])


def solution(mesh):
    placed = (P("comp", "pts"), P("pts", None), P("pts", None, None), P(), P("pts", None))
    return jax.shard_map(
        local, mesh=mesh, in_specs=placed, out_specs=P("comp", "pts"), check_vma=False
    )
```

time: 87.4 us -> 67.1 us (0.77)
  the two profiles are of different devices: /device:TPU:32 before, /device:TPU:1 now
where the time goes in v3:
time: 67.1 us; the launch traced here: 67 us
  Pallas kernels  63.1 us (94%)
  local copies, waits for them, and re-layouts  2.54 us (4%)
  other arithmetic  1.18 us (2%)
    pallas_call x1, Pallas kernels, whole(): pl.pallas_call(whole_kernel, out_shape=jax.ShapeDtypeStruct((CB, width),...  63.1 us
    unnamed x11, local copies, waits for them, and re-layouts  2.31 us

profile of v3, /device:TPU:1, one launch (start us, length us, event | category | flops | bytes accessed | tf_op | source)
XLA Modules:
  0.0 67.0 jit_solution(13357117493917099020)
XLA Ops:
  0.0 0.0 copy-start.4
  0.0 0.0 copy-start.3
  0.0 0.1 fusion.18
  0.1 0.1 divide_select_fusion
  0.2 0.5 copy-done.4
  0.7 0.1 constant_dynamic-slice_fusion
  0.8 0.2 subtract_reduce_fusion
  1.0 0.0 copy-done.3
  1.0 0.1 reduce
  1.1 0.0 copy-start.2
  1.1 0.3 convert_reduce_fusion
  1.4 0.0 copy-start
  1.4 0.2 select_reduce_fusion
  1.7 0.1 multiply_subtract_fusion
  1.8 0.3 copy-done.2
  2.0 0.1 fusion.2
  2.1 0.0 copy-start.1
  2.1 0.1 reshape.249.cell_ref
  2.3 0.2 copy-done
  2.5 0.6 copy-done.1
  3.1 63.1 %propagate_and_return.1 = bf16[9,13120]{1,0:T(8,128)(2,1)S(1)} custom-call(bf16[225,1152]{1,0:T(8,128)(2,1)S(1)} %copy-done, s32[8,3600]{1,0:T(8,128)S(1)} %copy-done.1, f32[8,128]{1,0:T(8,128)S(1)} %stack.10.coef_ref, s32[20608]{0:T(1024)S(1)} %reshape.249.cell_ref, s32[13312]{0:T(1024)S(1)} %pad.9.slot_ref), custom_call_target="tpu_custom_call" | custom-call | tf_op jit(solution)/shard_map/propagate_and_return/pallas_call | solution.py:305
  66.2 0.8 %copy.7 = bf16[9,13120]{1,0:T(8,128)(2,1)} copy(bf16[9,13120]{1,0:T(8,128)(2,1)S(1)} %propagate_and_return.1) | data formatting | bytes 472320
  (7 shorter events, 0.1 us)
Async XLA Ops:
  0.0 0.7 %copy-start.4 = (s32[16,16]{1,0:T(8,128)S(1)}, s32[16,16]{1,0:T(8,128)}, u32[]{:S(2)}) copy-start(s32[16,16]{1,0:T(8,128)} %param.8) | copy-start | bytes 3076
  0.0 1.0 %copy-start.3 = (s32[1,13120]{1,0:T(1,128)S(1)}, s32[1,13120]{1,0:T(1,128)}, u32[]{:S(2)}) copy-start(s32[1,13120]{1,0:T(1,128)} %param.9) | copy-start | bytes 157444
  1.1 0.9 %copy-start.2 = (s32[1,16,1280]{2,1,0:T(8,128)S(1)}, s32[1,16,1280]{2,1,0:T(8,128)}, u32[]{:S(2)}) copy-start(s32[1,16,1280]{2,1,0:T(8,128)} %param.7) | copy-start | bytes 245764
  1.4 1.1 %copy-start = (bf16[225,1152]{1,0:T(8,128)(2,1)S(1)}, bf16[225,1152]{1,0:T(8,128)(2,1)}, u32[]{:S(2)}) copy-start(bf16[225,1152]{1,0:T(8,128)(2,1)} %x_ref.1) | copy-start | bytes 1555204
  2.1 0.9 %copy-start.1 = (s32[8,3600]{1,0:T(8,128)S(1)}, s32[8,3600]{1,0:T(8,128)}, u32[]{:S(2)}) copy-start(s32[8,3600]{1,0:T(8,128)} %mask_ref.1) | copy-start | bytes 345604

commit v4 on v3

--- a/solution.py
+++ b/solution.py
@@ -55,31 +55,30 @@
     return row
 
 
-def spread_matrix(first, live):
+def spread_matrix(first, second, live):
     src = iota((LANES, 2 * LANES), 0)
     dst = iota((LANES, 2 * LANES), 1)
     half = dst // LANES
     lane2 = dst - half * LANES
     return one_hot(
-        jnp.logical_and(lane2 < live * CB, src == first + half * CB + lane2 - (lane2 // CB) * CB)
+        jnp.logical_and(lane2 < live * CB, src == jnp.where(half == 0, first, second) + lane2 - (lane2 // CB) * CB)
     )
 
 
 def partners(c):
     z = c // 2
-    order = []
-    for dist in (4, 3, 2, 1):
-        for chip in ((4,) if dist == 4 else (dist, 8 - dist)):
+    order = [z * 2 + 1 - (c - z * 2)]
+    for dist in (1, 2, 3, 4):
+        for chip in (4,) if dist == 4 else (dist, 8 - dist):
             for core in range(2):
                 order.append(lax.rem(z + chip, 8) * 2 + core)
-    order.append(z * 2 + 1 - (c - z * 2))
     return order
 
 
 def whole_kernel(
-    x_ref, mask_ref, coef_ref, cell_ref, slot_ref, out_ref,
-    sendbuf, piece, hsend, hrecv, ymid, mprev, mown, mnext, mstack, mexp, mdown, kbuf, va, vb,
-    vfin, tab, stage, outgo, income, cells, slots,
+    x_ref, mask_ref, coef_ref, cell_ref, count_ref, back_ref, out_ref,
+    xin, sendbuf, piece, hsend, hrecv, ymid, mprev, mown, mnext, mstack, mexp, mdown, kbuf, va, vb,
+    vfin, tab, stage, outgo, income, back, slotv, cells, counts, slots,
     s_send, s_recv, h_send, h_recv, m_send, m_recv, l_sem, o_send, o_recv,
 ):
     c = lax.axis_index("comp")
@@ -100,42 +99,42 @@
         pl.semaphore_signal(
             barrier, inc=1, device_id={"pts": lax.rem(j + s, NB)}, device_id_type=pl.DeviceIdType.MESH
         )
-    get_mask = pltpu.make_async_copy(mask_ref, mown, l_sem.at[1])
-    get_cells = pltpu.make_async_copy(cell_ref, cells, l_sem.at[2])
-    get_slots = pltpu.make_async_copy(slot_ref, slots, l_sem.at[3])
-    get_mask.start()
-    get_cells.start()
-    get_slots.start()
-
+    get_x = pltpu.make_async_copy(x_ref, xin, l_sem.at[1])
+    get_mask = pltpu.make_async_copy(mask_ref, mown, l_sem.at[2])
+    get_counts = pltpu.make_async_copy(count_ref, counts, l_sem.at[3])
+    get_back = pltpu.make_async_copy(back_ref, back, l_sem.at[4])
+    get_cells = pltpu.make_async_copy(cell_ref, cells.at[pl.ds(0, NB * CAP)], l_sem.at[5])
+    for get in (get_x, get_mask, get_counts, get_back, get_cells):
+        get.start()
     ymid[LB : 3 * SEG, :] = jnp.zeros((3 * SEG - LB, LANES), F32)
+    get_x.wait()
+    get_mask.wait()
+    pl.semaphore_wait(barrier, 2 * (NB - 1))
+
     m_id = iota((ROWS * NB * CB, LANES), 0)
     lane = iota((1, LANES), 1)
     pos = lane // CB
     lane_s = iota((SEG, LANES), 1)
-    x = x_ref[...]
-    for t in range(NB):
-        row = pos if t % 4 < 2 else ROWS - 1 - pos
+    x = xin[...]
+    copies = []
+    for n, t in enumerate(others + [c]):
+        row = jnp.where(lax.rem(t, 4) < 2, pos, ROWS - 1 - pos)
         want = jnp.where(lane < ROWS * CB, row * (NB * CB) + t * CB + lane - pos * CB, -1)
         ymid[0:LB, :] = mm(x, one_hot(m_id == want))
         y0 = ymid[0:SEG, :]
         y1 = pltpu.roll(ymid[SEG : 2 * SEG, :], 72, 1)
         y2 = pltpu.roll(ymid[2 * SEG : 3 * SEG, :], 16, 1)
-        sendbuf[t, :, 0:LANES] = jnp.where(lane_s < 72, y0, y1).astype(BF16)
-        sendbuf[t, :, LANES : 2 * LANES] = jnp.where(lane_s < 16, y1, y2).astype(BF16)
-
-    get_mask.wait()
-    pl.semaphore_wait(barrier, 2 * (NB - 1))
-
-    copies = []
-    for to in others:
-        copies.append(send(sendbuf.at[to], piece.at[c], s_send.at[to], s_recv.at[c], comp=to))
-        copies[-1].start()
-    m_up = send(mown, mprev, m_send.at[0], m_recv.at[0], pts=nxt)
-    m_up.start()
-    m_dn = send(mown, mnext, m_send.at[1], m_recv.at[1], pts=prv)
-    m_dn.start()
-    own = pltpu.make_async_copy(sendbuf.at[c], piece.at[c], l_sem.at[0])
-    own.start()
+        to = sendbuf if n < NB - 1 else piece
+        to[t, :, 0:LANES] = jnp.where(lane_s < 72, y0, y1).astype(BF16)
+        to[t, :, LANES : 2 * LANES] = jnp.where(lane_s < 16, y1, y2).astype(BF16)
+        if n < NB - 1:
+            copies.append(send(sendbuf.at[t], piece.at[c], s_send.at[t], s_recv.at[c], comp=t))
+            copies[-1].start()
+        if n == 1:
+            m_up = send(mown, mprev, m_send.at[0], m_recv.at[0], pts=nxt)
+            m_up.start()
+            m_dn = send(mown, mnext, m_send.at[1], m_recv.at[1], pts=prv)
+            m_dn.start()
 
     m_up.wait()
     m_dn.wait()
@@ -169,6 +168,32 @@
             1.0 - ax * lon_down - ad * mdown[i * step_rows : (i + 1) * step_rows, :]
         )
 
+    get_counts.wait()
+    get_back.wait()
+    width = out_ref.shape[1]
+    offsets = [jnp.int32(0)]
+    for i in range(NB - 1):
+        offsets.append(offsets[-1] + counts[i, j])
+    for a in range(0, width, SLOT_ROWS):
+        size = min(SLOT_ROWS, width - a)
+        picked = back[:, a : a + size]
+        start = jnp.zeros_like(picked)
+        place = jnp.zeros_like(picked)
+        for i in range(1, NB):
+            later = picked >= offsets[i]
+            start = jnp.where(later, offsets[i], start)
+            place = jnp.where(later, i * CAP_ROWS, place)
+        within = picked - start
+        place = place + within
+        for g in range(1, GROUPS):
+            place = place + jnp.where(within >= g * USED_ROWS, NB * CAP_ROWS - USED_ROWS, 0)
+        slotv[:, a : a + size] = place
+    slotv[:, width:] = jnp.zeros((1, SLOT_ROWS * SLOT_GROUPS - width), jnp.int32)
+    put_slots = pltpu.make_async_copy(slotv, slots, l_sem.at[0])
+    put_slots.start()
+    for i in range(USED_ROWS * GROUPS - CAP):
+        cells[NB * CAP + i] = 0
+
     src = iota((2 * LANES, LANES), 0)
     dst = iota((2 * LANES, LANES), 1)
     seg = dst // OWN
@@ -177,9 +202,7 @@
     )
     hops = []
     for b in [c] + others:
-        if not hops:
-            own.wait()
-        else:
+        if hops:
             send(sendbuf.at[b], piece.at[b], s_send.at[b], s_recv.at[b], comp=b).wait_recv()
         hsend[b] = mm(piece[b], h_pack).astype(BF16)
         hops.append(send(hsend.at[b], hrecv.at[b], h_send.at[b], h_recv.at[b], pts=down))
@@ -223,7 +246,9 @@
                 vfin[k : k + step_rows, :] = new.astype(BF16)
 
     for pair in range(ROWS // 2):
-        both = mm(vfin[...], spread_matrix(OWN + 2 * pair * CB, GROUPS))
+        here = jnp.where(north, 2 * pair, ROWS - 1 - 2 * pair)
+        then = jnp.where(north, 2 * pair + 1, ROWS - 2 - 2 * pair)
+        both = mm(vfin[...], spread_matrix(OWN + here * CB, OWN + then * CB, GROUPS))
         tab[2 * pair * LON : (2 * pair + 1) * LON, :] = both[:, :LANES]
         tab[(2 * pair + 1) * LON : (2 * pair + 2) * LON, :] = both[:, LANES:]
     get_cells.wait()
@@ -233,7 +258,7 @@
         def rows(q, _):
             for u in range(unroll):
                 r = q * unroll + u
-                at = cells.at[pl.ds(d * (USED_ROWS * GROUPS) + r, (GROUPS - 1) * USED_ROWS + 1)]
+                at = cells.at[pl.ds(d * CAP + r, (GROUPS - 1) * USED_ROWS + 1)]
                 stage[pl.ds(r, 1), :] = merge_rows(tab, at, GROUPS, USED_ROWS, lane)
             return 0
 
@@ -264,16 +289,16 @@
     total = NB * CAP_ROWS
     got = income[...].reshape(total, LANES)
     for pair in range(GROUPS // 2):
-        both = mm(got, spread_matrix(2 * pair * CB, SLOT_GROUPS))
+        both = mm(got, spread_matrix(2 * pair * CB, (2 * pair + 1) * CB, SLOT_GROUPS))
         tab[2 * pair * total : (2 * pair + 1) * total, :] = both[:, :LANES]
         tab[(2 * pair + 1) * total : (2 * pair + 2) * total, :] = both[:, LANES:]
-    get_slots.wait()
+    put_slots.wait()
     slot_unroll = 16
 
     def slot_rows(q, _):
         for u in range(slot_unroll):
             r = q * slot_unroll + u
-            at = slots.at[pl.ds(r, (SLOT_GROUPS - 1) * SLOT_ROWS + 1)]
+            at = slots.at[0, pl.ds(r, (SLOT_GROUPS - 1) * SLOT_ROWS + 1)]
             stage[pl.ds(r, 1), :] = merge_rows(tab, at, SLOT_GROUPS, SLOT_ROWS, lane)
         return 0
 
@@ -283,7 +308,6 @@
     group = t_row // 16
     comp = t_row - group * 16
     turn = one_hot(jnp.logical_and(comp < CB, t_lane == group * CB + comp))
-    width = out_ref.shape[1]
     turned = lax.dot_general(
         turn, stage[...].astype(BF16), (((1,), (1,)), ((), ())), preferred_element_type=F32
     )
@@ -297,17 +321,18 @@
         hop.wait_send()
 
 
-def whole(x, mask, coef, cell_idx, slot_idx, width):
+def whole(x, mask, coef, cells, counts, back):
     dma = pltpu.SemaphoreType.DMA
     vmem = pl.BlockSpec(memory_space=pltpu.VMEM)
     hbm = pl.BlockSpec(memory_space=pltpu.HBM)
     wrapped = PAD + LON + 8
     return pl.pallas_call(
         whole_kernel,
-        out_shape=jax.ShapeDtypeStruct((CB, width), BF16),
-        in_specs=[vmem, hbm, vmem, hbm, hbm],
+        out_shape=jax.ShapeDtypeStruct((CB, back.shape[1]), BF16),
+        in_specs=[hbm, hbm, vmem, hbm, hbm, hbm],
         out_specs=vmem,
         scratch_shapes=[
+            pltpu.VMEM(x.shape, BF16),
             pltpu.VMEM((NB, SEG, 2 * LANES), BF16),
             pltpu.VMEM((NB, SEG, 2 * LANES), BF16),
             pltpu.VMEM((NB, SEG, LANES), BF16),
@@ -327,16 +352,19 @@
             pltpu.VMEM((SLOT_ROWS, LANES), F32),
             pltpu.VMEM((NB, CAP_ROWS, LANES), BF16),
             pltpu.VMEM((NB, CAP_ROWS, LANES), BF16),
-            pltpu.SMEM(cell_idx.shape, jnp.int32),
-            pltpu.SMEM(slot_idx.shape, jnp.int32),
-            dma((NB,)), dma((NB,)), dma((NB,)), dma((NB,)), dma((2,)), dma((2,)), dma((4,)),
+            pltpu.VMEM(back.shape, jnp.int32),
+            pltpu.VMEM((1, SLOT_ROWS * SLOT_GROUPS), jnp.int32),
+            pltpu.SMEM((NB * CAP + USED_ROWS * GROUPS - CAP,), jnp.int32),
+            pltpu.SMEM((NB, NB), jnp.int32),
+            pltpu.SMEM((1, SLOT_ROWS * SLOT_GROUPS), jnp.int32),
+            dma((NB,)), dma((NB,)), dma((NB,)), dma((NB,)), dma((2,)), dma((2,)), dma((6,)),
             dma((NB,)), dma((NB,)),
         ],
         compiler_params=pltpu.CompilerParams(
             collective_id=0, has_side_effects=True, vmem_limit_bytes=52 << 20
         ),
         name="propagate_and_return",
-    )(x, mask, coef, cell_idx, slot_idx)
+    )(x, mask, coef, cells, counts, back)
 
 
 def coefficients(comp_here, pts_here):
@@ -372,26 +400,8 @@
 def local(spectra, land_mask, send_rows, row_counts, return_index):
     comp_here = lax.axis_index("comp")
     pts_here = lax.axis_index("pts")
-    north = comp_here % 4 < 2
-
-    cells = send_rows[0]
-    row = cells // LON
-    cell_row = jnp.where(north, row, ROWS - 1 - row) * LON + cells - row * LON
-    cell_idx = jnp.pad(cell_row, ((0, 0), (0, USED_ROWS * GROUPS - CAP))).reshape(-1)
-
-    counts_in = lax.dynamic_slice_in_dim(row_counts, pts_here, 1, 1)[:, 0]
-    offsets = jnp.cumsum(counts_in) - counts_in
-    picked = return_index[0]
-    source = jnp.sum((picked[:, None] >= offsets[None, :]).astype(jnp.int32), axis=1) - 1
-    start = jnp.sum(
-        jnp.where(source[:, None] == jnp.arange(NB, dtype=jnp.int32)[None, :], offsets[None, :], 0), axis=1
-    )
-    within = picked - start
-    group = within // USED_ROWS
-    slot = group * (NB * CAP_ROWS) + source * CAP_ROWS + within - group * USED_ROWS
-    slot_idx = jnp.pad(slot, (0, SLOT_ROWS * SLOT_GROUPS - slot.shape[0]))
     coef = coefficients(comp_here, pts_here)
-    return whole(spectra, land_mask, coef, cell_idx, slot_idx, picked.shape[0])
+    return whole(spectra, land_mask, coef, send_rows.reshape(-1), row_counts, return_index)
 
 
 def solution(mesh):

time: 67.1 us -> 65.6 us (0.978)
  the two profiles are of different devices: /device:TPU:1 before, /device:TPU:32 now
where the time goes in v4:
time: 65.6 us; the launch traced here: 64.7 us
  Pallas kernels  61.7 us (94%)
  local copies, waits for them, and re-layouts  2.75 us (4%)
    pallas_call x1, Pallas kernels, whole(): pl.pallas_call(whole_kernel, out_shape=jax.ShapeDtypeStruct((CB, back.sha...  61.7 us
    unnamed x9, local copies, waits for them, and re-layouts  1.81 us

profile of v4, /device:TPU:32, one launch (start us, length us, event | category | flops | bytes accessed | tf_op | source)
XLA Modules:
  0.0 64.7 jit_solution(3999593616216736181)
XLA Ops:
  0.0 0.0 copy-start.1
  0.0 0.1 fusion.11
  0.1 0.1 divide_select_fusion
  0.2 0.0 copy-start.2
  0.2 0.0 copy-start.3
  0.3 0.9 %reshape.217.cell_ref = s32[20480]{0:T(1024)S(1)} reshape(s32[1,16,1280]{2,1,0:T(8,128)} %param.7) | data formatting | bytes 163840 | tf_op jit(solution)/shard_map/reshape | solution.py:404
  1.2 0.0 copy-done.1
  1.2 0.0 copy-done.2
  1.2 0.0 copy-done.3
  1.2 0.0 copy-start
  1.2 1.0 %copy-done = bf16[225,1152]{1,0:T(8,128)(2,1)S(1)} copy-done((bf16[225,1152]{1,0:T(8,128)(2,1)S(1)}, bf16[225,1152]{1,0:T(8,128)(2,1)}, u32[]{:S(2)}) %copy-start) | copy-done | bytes 518424
  2.2 61.7 %propagate_and_return.1 = bf16[9,13120]{1,0:T(8,128)(2,1)S(1)} custom-call(bf16[225,1152]{1,0:T(8,128)(2,1)S(1)} %copy-done, s32[8,3600]{1,0:T(8,128)S(1)} %copy-done.1, f32[8,128]{1,0:T(8,128)S(1)} %stack.10.coef_ref, s32[20480]{0:T(1024)S(1)} %reshape.217.cell_ref, s32[16,16]{1,0:T(8,128)S(1)} %copy-done.3, s32[1,13120]{1,0:T(1,128)S(1)} %copy-done.2), custom_call_target="tpu_custom_call" | custom-call | tf_op jit(solution)/shard_map/propagate_and_return/pallas_call | solution.py:329
  63.9 0.8 %copy.7 = bf16[9,13120]{1,0:T(8,128)(2,1)} copy(bf16[9,13120]{1,0:T(8,128)(2,1)S(1)} %propagate_and_return.1) | data formatting | bytes 472320
  (3 shorter events, 0.0 us)
Async XLA Ops:
  0.0 1.2 %copy-start.1 = (s32[8,3600]{1,0:T(8,128)S(1)}, s32[8,3600]{1,0:T(8,128)}, u32[]{:S(2)}) copy-start(s32[8,3600]{1,0:T(8,128)} %mask_ref.1) | copy-start | bytes 345604
  0.2 0.9 %copy-start.2 = (s32[1,13120]{1,0:T(1,128)S(1)}, s32[1,13120]{1,0:T(1,128)}, u32[]{:S(2)}) copy-start(s32[1,13120]{1,0:T(1,128)} %back_ref.1) | copy-start | bytes 157444
  0.2 0.9 %copy-start.3 = (s32[16,16]{1,0:T(8,128)S(1)}, s32[16,16]{1,0:T(8,128)}, u32[]{:S(2)}) copy-start(s32[16,16]{1,0:T(8,128)} %count_ref.1) | copy-start | bytes 3076
  1.2 1.0 %copy-start = (bf16[225,1152]{1,0:T(8,128)(2,1)S(1)}, bf16[225,1152]{1,0:T(8,128)(2,1)}, u32[]{:S(2)}) copy-start(bf16[225,1152]{1,0:T(8,128)(2,1)} %x_ref.1) | copy-start | bytes 1555204

commit v5 on v4

--- a/solution.py
+++ b/solution.py
@@ -23,6 +23,9 @@
 CAP = 1280
 CAP_ROWS = 96
 USED_ROWS = 92
+PAIR_GROUPS = 7
+CELLS = 2048
+CHUNK = 720
 SLOT_ROWS = 1024
 SLOT_GROUPS = 13
 F32 = jnp.float32
@@ -48,10 +51,10 @@
     )
 
 
-def merge_rows(tab, at, groups, stride, lane):
+def merge_rows(tab, at, groups, stride, lane, width=CB):
     row = tab[pl.ds(at[0], 1), :]
     for g in range(1, groups):
-        row = jnp.where(lane >= CB * g, tab[pl.ds(at[g * stride], 1), :], row)
+        row = jnp.where(lane >= width * g, tab[pl.ds(at[g * stride], 1), :], row)
     return row
 
 
@@ -78,8 +81,8 @@
 def whole_kernel(
     x_ref, mask_ref, coef_ref, cell_ref, count_ref, back_ref, out_ref,
     xin, sendbuf, piece, hsend, hrecv, ymid, mprev, mown, mnext, mstack, mexp, mdown, kbuf, va, vb,
-    vfin, tab, stage, outgo, income, back, slotv, cells, counts, slots,
-    s_send, s_recv, h_send, h_recv, m_send, m_recv, l_sem, o_send, o_recv,
+    vfin, vmate, tab, stage, outgo, income, back, slotv, cells, counts, slots,
+    s_send, s_recv, h_send, h_recv, m_send, m_recv, l_sem, c_sem, v_send, v_recv, o_send, o_recv,
 ):
     c = lax.axis_index("comp")
     j = lax.axis_index("pts")
@@ -90,6 +93,8 @@
     east = jnp.logical_or(quad == 0, quad == 3)
     down = jnp.where(north, nxt, prv)
     others = partners(c)
+    core = lax.rem(c, 2)
+    mate = c + 1 - 2 * core
 
     barrier = pltpu.get_barrier_semaphore()
     for s in range(1, NB):
@@ -99,17 +104,23 @@
         pl.semaphore_signal(
             barrier, inc=1, device_id={"pts": lax.rem(j + s, NB)}, device_id_type=pl.DeviceIdType.MESH
         )
+        pl.semaphore_signal(
+            barrier, inc=1, device_id={"comp": mate, "pts": lax.rem(j + s, NB)},
+            device_id_type=pl.DeviceIdType.MESH,
+        )
     get_x = pltpu.make_async_copy(x_ref, xin, l_sem.at[1])
     get_mask = pltpu.make_async_copy(mask_ref, mown, l_sem.at[2])
     get_counts = pltpu.make_async_copy(count_ref, counts, l_sem.at[3])
     get_back = pltpu.make_async_copy(back_ref, back, l_sem.at[4])
-    get_cells = pltpu.make_async_copy(cell_ref, cells.at[pl.ds(0, NB * CAP)], l_sem.at[5])
-    for get in (get_x, get_mask, get_counts, get_back, get_cells):
+    get_cells = [
+        pltpu.make_async_copy(cell_ref.at[0, i], cells.at[pl.ds(i * CELLS, CAP)], c_sem.at[i]) for i in range(NB)
+    ]
+    for get in [get_x, get_mask, get_counts, get_back] + get_cells:
         get.start()
     ymid[LB : 3 * SEG, :] = jnp.zeros((3 * SEG - LB, LANES), F32)
     get_x.wait()
     get_mask.wait()
-    pl.semaphore_wait(barrier, 2 * (NB - 1))
+    pl.semaphore_wait(barrier, 3 * (NB - 1))
 
     m_id = iota((ROWS * NB * CB, LANES), 0)
     lane = iota((1, LANES), 1)
@@ -191,8 +202,10 @@
     slotv[:, width:] = jnp.zeros((1, SLOT_ROWS * SLOT_GROUPS - width), jnp.int32)
     put_slots = pltpu.make_async_copy(slotv, slots, l_sem.at[0])
     put_slots.start()
-    for i in range(USED_ROWS * GROUPS - CAP):
-        cells[NB * CAP + i] = 0
+    for i, get in enumerate(get_cells):
+        get.wait()
+        for k in range(CAP, USED_ROWS * GROUPS):
+            cells[i * CELLS + k] = 0
 
     src = iota((2 * LANES, LANES), 0)
     dst = iota((2 * LANES, LANES), 1)
@@ -228,6 +241,7 @@
             a = PAD + b * LB + t * SEG
             va[a : a + size, :] = full[:size, t * LANES : (t + 1) * LANES] * mexp[a : a + size, :]
 
+    shares = []
     for it in range(ITERS):
         v, w = (va, vb) if it % 2 == 0 else (vb, va)
         v[PAD - 1 : PAD, :] = v[PAD + LON - 1 : PAD + LON, :]
@@ -244,47 +258,111 @@
                 w[a : a + step_rows, :] = new
             else:
                 vfin[k : k + step_rows, :] = new.astype(BF16)
-
+                if (k + step_rows) % CHUNK == 0:
+                    n = k // CHUNK
+                    part = pl.ds(n * CHUNK, CHUNK)
+                    shares.append(send(vfin.at[part], vmate.at[part], v_send.at[n], v_recv.at[n], comp=mate))
+                    shares[-1].start()
+
+    spreads = []
     for pair in range(ROWS // 2):
+        src = iota((2 * LANES, 2 * LANES), 0)
+        dst = iota((2 * LANES, 2 * LANES), 1)
+        half = dst // LANES
+        lane2 = dst - half * LANES
+        part = lane2 - (lane2 // (2 * CB)) * (2 * CB)
+        of = part // CB
         here = jnp.where(north, 2 * pair, ROWS - 1 - 2 * pair)
         then = jnp.where(north, 2 * pair + 1, ROWS - 2 - 2 * pair)
-        both = mm(vfin[...], spread_matrix(OWN + here * CB, OWN + then * CB, GROUPS))
-        tab[2 * pair * LON : (2 * pair + 1) * LON, :] = both[:, :LANES]
-        tab[(2 * pair + 1) * LON : (2 * pair + 2) * LON, :] = both[:, LANES:]
-    get_cells.wait()
+        first = OWN + jnp.where(half == 0, here, then) * CB + jnp.where(of == core, 0, LANES)
+        spreads.append(
+            one_hot(jnp.logical_and(lane2 < PAIR_GROUPS * 2 * CB, src == first + part - of * CB))
+        )
+    for n, share in enumerate(shares):
+        share.wait_recv()
+        part = slice(n * CHUNK, (n + 1) * CHUNK)
+        values = jnp.concatenate([vfin[part, :], vmate[part, :]], axis=1)
+        for pair in range(ROWS // 2):
+            both = mm(values, spreads[pair])
+            a = 2 * pair * LON + n * CHUNK
+            tab[a : a + CHUNK, :] = both[:, :LANES]
+            tab[a + LON : a + LON + CHUNK, :] = both[:, LANES:]
     unroll = 23
-
-    def fill_block(d):
-        def rows(q, _):
-            for u in range(unroll):
-                r = q * unroll + u
-                at = cells.at[pl.ds(d * CAP + r, (GROUPS - 1) * USED_ROWS + 1)]
-                stage[pl.ds(r, 1), :] = merge_rows(tab, at, GROUPS, USED_ROWS, lane)
-            return 0
-
-        lax.fori_loop(0, USED_ROWS // unroll, rows, 0)
-
+    c_src = iota((2 * LANES, 2 * LANES), 0)
+    c_dst = iota((2 * LANES, 2 * LANES), 1)
+    c_core = c_dst // LANES
+    c_lane = c_dst - c_core * LANES
+    c_group = c_lane // CB
+    c_half = lax.rem(c_group, 2)
+    c_want = c_half * LANES + (c_group // 2) * (2 * CB) + c_core * CB + c_lane - c_group * CB
+    cut = one_hot(jnp.logical_and(c_group < GROUPS, c_src == c_want))
     stage[USED_ROWS:CAP_ROWS, :] = jnp.zeros((CAP_ROWS - USED_ROWS, LANES), F32)
+    stage[CAP_ROWS + USED_ROWS : 2 * CAP_ROWS, :] = jnp.zeros((CAP_ROWS - USED_ROWS, LANES), F32)
+    stride = 2 * USED_ROWS
+
+    def block_to(d, n):
+        return send(
+            outgo.at[d, n], income.at[j], o_send.at[d, n], o_recv.at[j],
+            comp=c - core + n, pts=d,
+        )
 
     def owner(s, _):
-        d = lax.rem(j + s, NB)
-        fill_block(d)
-        outgo[d] = stage[0:CAP_ROWS, :].astype(BF16)
-        send(outgo.at[d], income.at[j], o_send.at[d], o_recv.at[j], pts=d).start()
+        d = lax.rem(j + 2 * lax.rem(s, NB // 2) + core, NB)
+        for half in range(2):
+
+            def rows(q, _, half=half):
+                for u in range(unroll):
+                    r = q * unroll + u
+                    at = cells.at[pl.ds(d * CELLS + half * USED_ROWS + r, (PAIR_GROUPS - 1) * stride + 1)]
+                    stage[pl.ds(half * CAP_ROWS + r, 1), :] = merge_rows(
+                        tab, at, PAIR_GROUPS, stride, lane, 2 * CB
+                    )
+                return 0
+
+            lax.fori_loop(0, USED_ROWS // unroll, rows, 0)
+        packed = jnp.concatenate([stage[0:CAP_ROWS, :], stage[CAP_ROWS : 2 * CAP_ROWS, :]], axis=1)
+        blocks = mm(packed.astype(BF16), cut).astype(BF16)
+
+        @pl.when(d != j)
+        def _():
+            for n in range(2):
+                outgo[d, n] = blocks[:, n * LANES : (n + 1) * LANES]
+                block_to(d, n).start()
+
+        @pl.when(d == j)
+        def _():
+            income[j] = blocks[:, :LANES]
+            outgo[d, 1] = blocks[:, LANES:]
+            block_to(d, 1).start()
+
         return 0
 
-    lax.fori_loop(1, NB, owner, 0)
-    fill_block(j)
-    income[j] = stage[0:CAP_ROWS, :].astype(BF16)
+    lax.fori_loop(1, NB // 2 + 1, owner, 0)
+
+    def sent(s, _):
+        d = lax.rem(j + 2 * s + core, NB)
+        block_to(d, 1).wait_send()
+
+        @pl.when(d != j)
+        def _():
+            block_to(d, 0).wait_send()
+
+        return 0
+
+    lax.fori_loop(0, NB // 2, sent, 0)
 
     def arrive(s, _):
         d = lax.rem(j + s, NB)
-        copy = send(outgo.at[d], income.at[d], o_send.at[d], o_recv.at[d], pts=d)
-        copy.wait_send()
-        copy.wait_recv()
+
+        @pl.when(jnp.logical_or(s > 0, core == 1))
+        def _():
+            send(
+                outgo.at[d, 0], income.at[d], o_send.at[d, 0], o_recv.at[d], comp=mate, pts=d
+            ).wait_recv()
+
         return 0
 
-    lax.fori_loop(1, NB, arrive, 0)
+    lax.fori_loop(0, NB, arrive, 0)
 
     total = NB * CAP_ROWS
     got = income[...].reshape(total, LANES)
@@ -315,7 +393,7 @@
         size = min(SLOT_ROWS, width - g * SLOT_ROWS)
         out_ref[:, g * SLOT_ROWS : g * SLOT_ROWS + size] = turned[16 * g : 16 * g + CB, :size].astype(BF16)
 
-    for copy in copies:
+    for copy in copies + shares:
         copy.wait_send()
     for hop in hops:
         hop.wait_send()
@@ -348,20 +426,21 @@
             pltpu.VMEM((wrapped, LANES), F32),
             pltpu.VMEM((wrapped, LANES), F32),
             pltpu.VMEM((LON, LANES), BF16),
+            pltpu.VMEM((LON, LANES), BF16),
             pltpu.VMEM((ROWS * LON, LANES), F32),
             pltpu.VMEM((SLOT_ROWS, LANES), F32),
-            pltpu.VMEM((NB, CAP_ROWS, LANES), BF16),
+            pltpu.VMEM((NB, 2, CAP_ROWS, LANES), BF16),
             pltpu.VMEM((NB, CAP_ROWS, LANES), BF16),
             pltpu.VMEM(back.shape, jnp.int32),
             pltpu.VMEM((1, SLOT_ROWS * SLOT_GROUPS), jnp.int32),
-            pltpu.SMEM((NB * CAP + USED_ROWS * GROUPS - CAP,), jnp.int32),
+            pltpu.SMEM((NB * CELLS,), jnp.int32),
             pltpu.SMEM((NB, NB), jnp.int32),
             pltpu.SMEM((1, SLOT_ROWS * SLOT_GROUPS), jnp.int32),
-            dma((NB,)), dma((NB,)), dma((NB,)), dma((NB,)), dma((2,)), dma((2,)), dma((6,)),
-            dma((NB,)), dma((NB,)),
+            dma((NB,)), dma((NB,)), dma((NB,)), dma((NB,)), dma((2,)), dma((2,)), dma((6,)), dma((NB,)),
+            dma((LON // CHUNK,)), dma((LON // CHUNK,)), dma((NB, 2)), dma((NB,)),
         ],
         compiler_params=pltpu.CompilerParams(
-            collective_id=0, has_side_effects=True, vmem_limit_bytes=52 << 20
+            collective_id=0, has_side_effects=True, vmem_limit_bytes=60 << 20
         ),
         name="propagate_and_return",
     )(x, mask, coef, cells, counts, back)
@@ -401,7 +480,7 @@
     comp_here = lax.axis_index("comp")
     pts_here = lax.axis_index("pts")
     coef = coefficients(comp_here, pts_here)
-    return whole(spectra, land_mask, coef, send_rows.reshape(-1), row_counts, return_index)
+    return whole(spectra, land_mask, coef, send_rows, row_counts, return_index)
 
 
 def solution(mesh):

time: 65.6 us -> 66.8 us (1.018)
  Pallas kernels: 61.7 us -> 63.8 us
    pallas_call x1, Pallas kernels: 61.7 us -> 63.8 us  [whole(): pl.pallas_call(whole_kernel, out_shape=jax.ShapeDtypeStruct((CB, back.sha...]
    reshape x1 -> x0, local copies, waits for them, and re-layouts: 0.91 us -> none  [local(): send_rows.reshape(-1)]
    unnamed x9 -> x1, local copies, waits for them, and re-layouts: 1.81 us -> 1.79 us
where the time goes in v5:
time: 66.8 us; the launch traced here: 66.4 us
  Pallas kernels  63.8 us (96%)
  local copies, waits for them, and re-layouts  2.4 us (4%)
    pallas_call x1, Pallas kernels, whole(): pl.pallas_call(whole_kernel, out_shape=jax.ShapeDtypeStruct((CB, back.sha...  63.8 us
    unnamed x1, local copies, waits for them, and re-layouts  1.79 us

profile of v5, /device:TPU:32, one launch (start us, length us, event | category | flops | bytes accessed | tf_op | source)
XLA Modules:
  0.0 66.4 jit_solution(7454501339884942015)
XLA Ops:
  0.0 0.1 fusion.11
  0.1 0.1 divide_select_fusion
  0.2 0.6 stack.10.coef_ref
  0.8 63.8 %propagate_and_return.1 = bf16[9,13120]{1,0:T(8,128)(2,1)} custom-call(bf16[225,1152]{1,0:T(8,128)(2,1)} %x_ref.1, s32[8,3600]{1,0:T(8,128)} %mask_ref.1, f32[8,128]{1,0:T(8,128)} %stack.10.coef_ref, s32[1,16,1280]{2,1,0:T(8,128)} %cell_ref.1, s32[16,16]{1,0:T(8,128)} %count_ref.1, s32[1,13120]{1,0:T(1,128)} %back_ref.1), custom_call_target="tpu_custom_call" | custom-call | tf_op jit(solution)/shard_map/propagate_and_return/pallas_call | solution.py:407
  64.6 1.8 %copy.7 = bf16[9,13120]{1,0:T(8,128)(2,1)} copy(bf16[9,13120]{1,0:T(8,128)(2,1)} %propagate_and_return.1) | data formatting | bytes 472320
  (2 shorter events, 0.0 us)

commit v6 on v5

--- a/solution.py
+++ b/solution.py
@@ -18,7 +18,7 @@
 LB = 225
 SEG = 80
 NB = 16
-PAD = 8
+PAD = 16
 GROUPS = 14
 CAP = 1280
 CAP_ROWS = 96
@@ -68,6 +68,11 @@
     )
 
 
+def wrap(ref):
+    ref[0:PAD, :] = ref[LON : LON + PAD, :]
+    ref[PAD + LON : 2 * PAD + LON, :] = ref[PAD : 2 * PAD, :]
+
+
 def partners(c):
     z = c // 2
     order = [z * 2 + 1 - (c - z * 2)]
@@ -80,8 +85,8 @@
 
 def whole_kernel(
     x_ref, mask_ref, coef_ref, cell_ref, count_ref, back_ref, out_ref,
-    xin, sendbuf, piece, hsend, hrecv, ymid, mprev, mown, mnext, mstack, mexp, mdown, kbuf, va, vb,
-    vfin, vmate, tab, stage, outgo, income, back, slotv, cells, counts, slots,
+    xin, sendbuf, piece, hsend, hrecv, ymid, mprev, mown, mnext, mstack, mexp, mdown, kbuf, va, vb, vc,
+    vfin, vmate, tab, stage_a, stage_b, stage, outgo, income, back, slotv, cells, counts, slots,
     s_send, s_recv, h_send, h_recv, m_send, m_recv, l_sem, c_sem, v_send, v_recv, o_send, o_recv,
 ):
     c = lax.axis_index("comp")
@@ -96,56 +101,69 @@
     core = lax.rem(c, 2)
     mate = c + 1 - 2 * core
 
-    barrier = pltpu.get_barrier_semaphore()
-    for s in range(1, NB):
-        pl.semaphore_signal(
-            barrier, inc=1, device_id={"comp": lax.rem(c + s, NB)}, device_id_type=pl.DeviceIdType.MESH
-        )
-        pl.semaphore_signal(
-            barrier, inc=1, device_id={"pts": lax.rem(j + s, NB)}, device_id_type=pl.DeviceIdType.MESH
-        )
-        pl.semaphore_signal(
-            barrier, inc=1, device_id={"comp": mate, "pts": lax.rem(j + s, NB)},
-            device_id_type=pl.DeviceIdType.MESH,
-        )
     get_x = pltpu.make_async_copy(x_ref, xin, l_sem.at[1])
     get_mask = pltpu.make_async_copy(mask_ref, mown, l_sem.at[2])
+    get_x.start()
+    get_mask.start()
+
+    barrier = pltpu.get_barrier_semaphore()
+
+    def greet(**where):
+        pl.semaphore_signal(barrier, inc=1, device_id=where, device_id_type=pl.DeviceIdType.MESH)
+
+    for other in others:
+        greet(comp=other)
+    greet(pts=nxt)
+    greet(pts=prv)
+    for s in range(1, NB):
+        greet(comp=c - core + s % 2, pts=lax.rem(j + NB - s, NB))
     get_counts = pltpu.make_async_copy(count_ref, counts, l_sem.at[3])
     get_back = pltpu.make_async_copy(back_ref, back, l_sem.at[4])
     get_cells = [
         pltpu.make_async_copy(cell_ref.at[0, i], cells.at[pl.ds(i * CELLS, CAP)], c_sem.at[i]) for i in range(NB)
     ]
-    for get in [get_x, get_mask, get_counts, get_back] + get_cells:
-        get.start()
-    ymid[LB : 3 * SEG, :] = jnp.zeros((3 * SEG - LB, LANES), F32)
+    for n in range(2):
+        ymid[n, LB : 3 * SEG, :] = jnp.zeros((3 * SEG - LB, 2 * LANES), F32)
     get_x.wait()
     get_mask.wait()
-    pl.semaphore_wait(barrier, 3 * (NB - 1))
-
-    m_id = iota((ROWS * NB * CB, LANES), 0)
+    pl.semaphore_wait(barrier, NB + 1 + NB - 2 + 2 * core)
+
+    m_id = iota((ROWS * NB * CB, 2 * LANES), 0)
     lane = iota((1, LANES), 1)
-    pos = lane // CB
+    lane_2 = iota((1, 2 * LANES), 1)
+    lane_c = lane_2 // LANES
+    lane_1 = lane_2 - lane_c * LANES
+    pos = lane_1 // CB
     lane_s = iota((SEG, LANES), 1)
     x = xin[...]
     copies = []
-    for n, t in enumerate(others + [c]):
-        row = jnp.where(lax.rem(t, 4) < 2, pos, ROWS - 1 - pos)
-        want = jnp.where(lane < ROWS * CB, row * (NB * CB) + t * CB + lane - pos * CB, -1)
-        ymid[0:LB, :] = mm(x, one_hot(m_id == want))
-        y0 = ymid[0:SEG, :]
-        y1 = pltpu.roll(ymid[SEG : 2 * SEG, :], 72, 1)
-        y2 = pltpu.roll(ymid[2 * SEG : 3 * SEG, :], 16, 1)
-        to = sendbuf if n < NB - 1 else piece
-        to[t, :, 0:LANES] = jnp.where(lane_s < 72, y0, y1).astype(BF16)
-        to[t, :, LANES : 2 * LANES] = jnp.where(lane_s < 16, y1, y2).astype(BF16)
-        if n < NB - 1:
+    for n in range(NB // 2):
+        pair = [mate, c] if n == 0 else others[2 * n - 1 : 2 * n + 1]
+        chip = pair[0] // 2
+        row = jnp.where(lax.rem(chip, 2) == 0, pos, ROWS - 1 - pos)
+        want = row * (NB * CB) + (2 * chip + lane_c) * CB + lane_1 - pos * CB
+        want = jnp.where(lane_1 < ROWS * CB, want, -1)
+        y = ymid.at[n % 2]
+        y[0:LB, :] = mm(x, one_hot(m_id == want))
+        for k in range(2):
+            t = 2 * chip + k
+            cols = slice(k * LANES, (k + 1) * LANES)
+            y0 = y[0:SEG, cols]
+            y1 = pltpu.roll(y[SEG : 2 * SEG, cols], 72, 1)
+            y2 = pltpu.roll(y[2 * SEG : 3 * SEG, cols], 16, 1)
+            sendbuf[t, :, 0:LANES] = jnp.where(lane_s < 72, y0, y1).astype(BF16)
+            sendbuf[t, :, LANES : 2 * LANES] = jnp.where(lane_s < 16, y1, y2).astype(BF16)
+        for t in pair[:1] if n == 0 else pair:
             copies.append(send(sendbuf.at[t], piece.at[c], s_send.at[t], s_recv.at[c], comp=t))
             copies[-1].start()
-        if n == 1:
+        if n == 0:
             m_up = send(mown, mprev, m_send.at[0], m_recv.at[0], pts=nxt)
             m_up.start()
             m_dn = send(mown, mnext, m_send.at[1], m_recv.at[1], pts=prv)
             m_dn.start()
+            piece[c] = sendbuf[c]
+    for get in [get_counts, get_back] + get_cells:
+        get.start()
 
     m_up.wait()
     m_dn.wait()
@@ -163,8 +181,7 @@
     both = lax.dot_general(stack, e_both, (((0,), (0,)), ((), ())), preferred_element_type=F32)
     mexp[PAD : PAD + LON, :] = both[:, :LANES]
     mdown[...] = both[:, LANES:]
-    mexp[PAD - 1 : PAD, :] = mexp[PAD + LON - 1 : PAD + LON, :]
-    mexp[PAD + LON : PAD + LON + 1, :] = mexp[PAD : PAD + 1, :]
+    wrap(mexp)
     ax = coef_ref[0:1, :]
     ay = coef_ref[1:2, :]
     ad = coef_ref[2:3, :]
@@ -175,9 +192,10 @@
         lon_down = jnp.where(
             east, mexp[a + 1 : a + 1 + step_rows, :], mexp[a - 1 : a - 1 + step_rows, :]
         )
-        kbuf[i * step_rows : (i + 1) * step_rows, :] = m * (
+        kbuf[a : a + step_rows, :] = m * (
             1.0 - ax * lon_down - ad * mdown[i * step_rows : (i + 1) * step_rows, :]
         )
+    wrap(kbuf)
 
     get_counts.wait()
     get_back.wait()
@@ -241,28 +259,32 @@
             a = PAD + b * LB + t * SEG
             va[a : a + size, :] = full[:size, t * LANES : (t + 1) * LANES] * mexp[a : a + size, :]
 
+    wrap(va)
+    wide = CHUNK + 16
+    for w in (vb, vc):
+        w[0:8, :] = jnp.zeros((8, LANES), F32)
+        w[8 + wide : 16 + wide, :] = jnp.zeros((8, LANES), F32)
     shares = []
-    for it in range(ITERS):
-        v, w = (va, vb) if it % 2 == 0 else (vb, va)
-        v[PAD - 1 : PAD, :] = v[PAD + LON - 1 : PAD + LON, :]
-        v[PAD + LON : PAD + LON + 1, :] = v[PAD : PAD + 1, :]
-        for i in range(LON // step_rows):
-            a = PAD + i * step_rows
-            k = i * step_rows
-            here = v[a : a + step_rows, :]
-            side = jnp.where(east, v[a - 1 : a - 1 + step_rows, :], v[a + 1 : a + 1 + step_rows, :])
-            new = kbuf[k : k + step_rows, :] * here + mexp[a : a + step_rows, :] * (
-                ax * side + ay * pltpu.roll(here, CB, 1)
-            )
-            if it < ITERS - 1:
-                w[a : a + step_rows, :] = new
-            else:
-                vfin[k : k + step_rows, :] = new.astype(BF16)
-                if (k + step_rows) % CHUNK == 0:
-                    n = k // CHUNK
-                    part = pl.ds(n * CHUNK, CHUNK)
-                    shares.append(send(vfin.at[part], vmate.at[part], v_send.at[n], v_recv.at[n], comp=mate))
-                    shares[-1].start()
+    for n in range(LON // CHUNK):
+        first = PAD + n * CHUNK - 16
+        for it in range(ITERS):
+            v, w = ((va, vb), (vb, vc), (vc, vb), (vb, None))[it]
+            low, size, block = (8, wide, wide // 4) if it < ITERS - 1 else (16, CHUNK, CHUNK // 6)
+            for a in range(low, low + size, block):
+                at = a + first if it == 0 else a
+                here = v[at : at + block, :]
+                side = jnp.where(east, v[at - 1 : at - 1 + block, :], v[at + 1 : at + 1 + block, :])
+                new = kbuf[a + first : a + first + block, :] * here + mexp[a + first : a + first + block, :] * (
+                    ax * side + ay * pltpu.roll(here, CB, 1)
+                )
+                if it < ITERS - 1:
+                    w[a : a + block, :] = new
+                else:
+                    k = n * CHUNK + a - low
+                    vfin[k : k + block, :] = new.astype(BF16)
+        part = pl.ds(n * CHUNK, CHUNK)
+        shares.append(send(vfin.at[part], vmate.at[part], v_send.at[n], v_recv.at[n], comp=mate))
+        shares[-1].start()
 
     spreads = []
     for pair in range(ROWS // 2):
@@ -287,7 +309,6 @@
             a = 2 * pair * LON + n * CHUNK
             tab[a : a + CHUNK, :] = both[:, :LANES]
             tab[a + LON : a + LON + CHUNK, :] = both[:, LANES:]
-    unroll = 23
     c_src = iota((2 * LANES, 2 * LANES), 0)
     c_dst = iota((2 * LANES, 2 * LANES), 1)
     c_core = c_dst // LANES
@@ -296,8 +317,9 @@
     c_half = lax.rem(c_group, 2)
     c_want = c_half * LANES + (c_group // 2) * (2 * CB) + c_core * CB + c_lane - c_group * CB
     cut = one_hot(jnp.logical_and(c_group < GROUPS, c_src == c_want))
-    stage[USED_ROWS:CAP_ROWS, :] = jnp.zeros((CAP_ROWS - USED_ROWS, LANES), F32)
-    stage[CAP_ROWS + USED_ROWS : 2 * CAP_ROWS, :] = jnp.zeros((CAP_ROWS - USED_ROWS, LANES), F32)
+    for ref in (stage_a, stage_b):
+        for half in range(2):
+            ref[half, USED_ROWS:CAP_ROWS, :] = jnp.zeros((CAP_ROWS - USED_ROWS, LANES), F32)
     stride = 2 * USED_ROWS
 
     def block_to(d, n):
@@ -306,38 +328,50 @@
             comp=c - core + n, pts=d,
         )
 
-    def owner(s, _):
+    def gather(ref, s):
         d = lax.rem(j + 2 * lax.rem(s, NB // 2) + core, NB)
+        at_d = cells.at[pl.ds(pl.multiple_of(d * CELLS, CELLS), CELLS)]
         for half in range(2):
-
-            def rows(q, _, half=half):
-                for u in range(unroll):
-                    r = q * unroll + u
-                    at = cells.at[pl.ds(d * CELLS + half * USED_ROWS + r, (PAIR_GROUPS - 1) * stride + 1)]
-                    stage[pl.ds(half * CAP_ROWS + r, 1), :] = merge_rows(
-                        tab, at, PAIR_GROUPS, stride, lane, 2 * CB
-                    )
-                return 0
-
-            lax.fori_loop(0, USED_ROWS // unroll, rows, 0)
-        packed = jnp.concatenate([stage[0:CAP_ROWS, :], stage[CAP_ROWS : 2 * CAP_ROWS, :]], axis=1)
-        blocks = mm(packed.astype(BF16), cut).astype(BF16)
-
-        @pl.when(d != j)
-        def _():
-            for n in range(2):
-                outgo[d, n] = blocks[:, n * LANES : (n + 1) * LANES]
-                block_to(d, n).start()
-
-        @pl.when(d == j)
-        def _():
-            income[j] = blocks[:, :LANES]
-            outgo[d, 1] = blocks[:, LANES:]
-            block_to(d, 1).start()
-
+            for r in range(USED_ROWS):
+                at = at_d.at[pl.ds(half * USED_ROWS + r, (PAIR_GROUPS - 1) * stride + 1)]
+                ref[half, r : r + 1, :] = merge_rows(tab, at, PAIR_GROUPS, stride, lane, 2 * CB)
+
+    def blocks_of(ref):
+        packed = jnp.concatenate([ref[0], ref[1]], axis=1)
+        return mm(packed.astype(BF16), cut).astype(BF16)
+
+    def flush(ref, s):
+        d = lax.rem(j + 2 * s + core, NB)
+        blocks = blocks_of(ref)
+        for n in range(2):
+            outgo[d, n] = blocks[:, n * LANES : (n + 1) * LANES]
+            block_to(d, n).start()
+
+    gather(stage_a, 1)
+
+    def two_owners(q, _):
+        gather(stage_b, 2 * q + 2)
+        flush(stage_a, 2 * q + 1)
+        gather(stage_a, 2 * q + 3)
+        flush(stage_b, 2 * q + 2)
         return 0
 
-    lax.fori_loop(1, NB // 2 + 1, owner, 0)
+    lax.fori_loop(0, NB // 4 - 1, two_owners, 0)
+    gather(stage_b, NB // 2)
+    flush(stage_a, NB // 2 - 1)
+    last = lax.rem(j + core, NB)
+    blocks = blocks_of(stage_b)
+    outgo[last, 1] = blocks[:, LANES:]
+    block_to(last, 1).start()
+
+    @pl.when(core == 1)
+    def _():
+        outgo[last, 0] = blocks[:, :LANES]
+        block_to(last, 0).start()
+
+    @pl.when(core == 0)
+    def _():
+        income[j] = blocks[:, :LANES]
 
     def sent(s, _):
         d = lax.rem(j + 2 * s + core, NB)
@@ -371,7 +405,7 @@
         tab[2 * pair * total : (2 * pair + 1) * total, :] = both[:, :LANES]
         tab[(2 * pair + 1) * total : (2 * pair + 2) * total, :] = both[:, LANES:]
     put_slots.wait()
-    slot_unroll = 16
+    slot_unroll = 32
 
     def slot_rows(q, _):
         for u in range(slot_unroll):
@@ -403,7 +437,8 @@
     dma = pltpu.SemaphoreType.DMA
     vmem = pl.BlockSpec(memory_space=pltpu.VMEM)
     hbm = pl.BlockSpec(memory_space=pltpu.HBM)
-    wrapped = PAD + LON + 8
+    wrapped = PAD + LON + PAD
+    chunk = CHUNK + 32
     return pl.pallas_call(
         whole_kernel,
         out_shape=jax.ShapeDtypeStruct((CB, back.shape[1]), BF16),
@@ -415,19 +450,22 @@
             pltpu.VMEM((NB, SEG, 2 * LANES), BF16),
             pltpu.VMEM((NB, SEG, LANES), BF16),
             pltpu.VMEM((NB, SEG, LANES), BF16),
-            pltpu.VMEM((3 * SEG, LANES), F32),
+            pltpu.VMEM((2, 3 * SEG, 2 * LANES), F32),
             pltpu.VMEM((ROWS, LON), jnp.int32),
             pltpu.VMEM((ROWS, LON), jnp.int32),
             pltpu.VMEM((ROWS, LON), jnp.int32),
             pltpu.VMEM((3 * ROWS, LON), F32),
             pltpu.VMEM((wrapped, LANES), F32),
             pltpu.VMEM((LON, LANES), F32),
-            pltpu.VMEM((LON, LANES), F32),
             pltpu.VMEM((wrapped, LANES), F32),
             pltpu.VMEM((wrapped, LANES), F32),
+            pltpu.VMEM((chunk, LANES), F32),
+            pltpu.VMEM((chunk, LANES), F32),
             pltpu.VMEM((LON, LANES), BF16),
             pltpu.VMEM((LON, LANES), BF16),
             pltpu.VMEM((ROWS * LON, LANES), F32),
+            pltpu.VMEM((2, CAP_ROWS, LANES), F32),
+            pltpu.VMEM((2, CAP_ROWS, LANES), F32),
             pltpu.VMEM((SLOT_ROWS, LANES), F32),
             pltpu.VMEM((NB, 2, CAP_ROWS, LANES), BF16),
             pltpu.VMEM((NB, CAP_ROWS, LANES), BF16),

time: 66.8 us -> 68.6 us (1.027)
  Pallas kernels: 63.8 us -> 65.8 us
    pallas_call x1, Pallas kernels: 63.8 us -> 65.8 us  [whole(): pl.pallas_call(whole_kernel, out_shape=jax.ShapeDtypeStruct((CB, back.sha...]
where the time goes in v6:
time: 68.6 us; the launch traced here: 68.4 us
  Pallas kernels  65.8 us (96%)
  local copies, waits for them, and re-layouts  2.4 us (3%)
    pallas_call x1, Pallas kernels, whole(): pl.pallas_call(whole_kernel, out_shape=jax.ShapeDtypeStruct((CB, back.sha...  65.8 us
    unnamed x1, local copies, waits for them, and re-layouts  1.79 us

profile of v6, /device:TPU:32, one launch (start us, length us, event | category | flops | bytes accessed | tf_op | source)
XLA Modules:
  0.0 68.4 jit_solution(2663627264304462363)
XLA Ops:
  0.0 0.1 fusion.11
  0.1 0.1 divide_select_fusion
  0.2 0.6 stack.10.coef_ref
  0.8 65.8 %propagate_and_return.1 = bf16[9,13120]{1,0:T(8,128)(2,1)} custom-call(bf16[225,1152]{1,0:T(8,128)(2,1)} %x_ref.1, s32[8,3600]{1,0:T(8,128)} %mask_ref.1, f32[8,128]{1,0:T(8,128)} %stack.10.coef_ref, s32[1,16,1280]{2,1,0:T(8,128)} %cell_ref.1, s32[16,16]{1,0:T(8,128)} %count_ref.1, s32[1,13120]{1,0:T(1,128)} %back_ref.1), custom_call_target="tpu_custom_call" | custom-call | tf_op jit(solution)/shard_map/propagate_and_return/pallas_call | solution.py:442
  66.7 1.8 %copy.7 = bf16[9,13120]{1,0:T(8,128)(2,1)} copy(bf16[9,13120]{1,0:T(8,128)(2,1)} %propagate_and_return.1) | data formatting | bytes 472320
  (2 shorter events, 0.0 us)

commit v7 on v6

--- a/solution.py
+++ b/solution.py
@@ -86,7 +86,7 @@
 def whole_kernel(
     x_ref, mask_ref, coef_ref, cell_ref, count_ref, back_ref, out_ref,
     xin, sendbuf, piece, hsend, hrecv, ymid, mprev, mown, mnext, mstack, mexp, mdown, kbuf, va, vb, vc,
-    vfin, vmate, tab, stage_a, stage_b, stage, outgo, income, back, slotv, cells, counts, slots,
+    vfin, vmate, tab, stage, outgo, income, back, slotv, cells, counts, slots,
     s_send, s_recv, h_send, h_recv, m_send, m_recv, l_sem, c_sem, v_send, v_recv, o_send, o_recv,
 ):
     c = lax.axis_index("comp")
@@ -317,10 +317,11 @@
     c_half = lax.rem(c_group, 2)
     c_want = c_half * LANES + (c_group // 2) * (2 * CB) + c_core * CB + c_lane - c_group * CB
     cut = one_hot(jnp.logical_and(c_group < GROUPS, c_src == c_want))
-    for ref in (stage_a, stage_b):
-        for half in range(2):
-            ref[half, USED_ROWS:CAP_ROWS, :] = jnp.zeros((CAP_ROWS - USED_ROWS, LANES), F32)
+    for half in range(2):
+        a = half * CAP_ROWS + USED_ROWS
+        stage[a : a + CAP_ROWS - USED_ROWS, :] = jnp.zeros((CAP_ROWS - USED_ROWS, LANES), F32)
     stride = 2 * USED_ROWS
+    unroll = USED_ROWS // 2
 
     def block_to(d, n):
         return send(
@@ -328,39 +329,30 @@
             comp=c - core + n, pts=d,
         )
 
-    def gather(ref, s):
-        d = lax.rem(j + 2 * lax.rem(s, NB // 2) + core, NB)
-        at_d = cells.at[pl.ds(pl.multiple_of(d * CELLS, CELLS), CELLS)]
-        for half in range(2):
-            for r in range(USED_ROWS):
-                at = at_d.at[pl.ds(half * USED_ROWS + r, (PAIR_GROUPS - 1) * stride + 1)]
-                ref[half, r : r + 1, :] = merge_rows(tab, at, PAIR_GROUPS, stride, lane, 2 * CB)
-
-    def blocks_of(ref):
-        packed = jnp.concatenate([ref[0], ref[1]], axis=1)
+    def gather(d):
+        def rows(q, _):
+            base = d * CELLS + q * unroll
+            to = q * unroll + (q // 2) * (CAP_ROWS - USED_ROWS)
+            for u in range(unroll):
+                at = cells.at[pl.ds(base + u, (PAIR_GROUPS - 1) * stride + 1)]
+                stage[pl.ds(to + u, 1), :] = merge_rows(tab, at, PAIR_GROUPS, stride, lane, 2 * CB)
+            return 0
+
+        lax.fori_loop(0, 4, rows, 0)
+        packed = jnp.concatenate([stage[0:CAP_ROWS, :], stage[CAP_ROWS : 2 * CAP_ROWS, :]], axis=1)
         return mm(packed.astype(BF16), cut).astype(BF16)
 
-    def flush(ref, s):
+    def owner(s, _):
         d = lax.rem(j + 2 * s + core, NB)
-        blocks = blocks_of(ref)
+        blocks = gather(d)
         for n in range(2):
             outgo[d, n] = blocks[:, n * LANES : (n + 1) * LANES]
             block_to(d, n).start()
-
-    gather(stage_a, 1)
-
-    def two_owners(q, _):
-        gather(stage_b, 2 * q + 2)
-        flush(stage_a, 2 * q + 1)
-        gather(stage_a, 2 * q + 3)
-        flush(stage_b, 2 * q + 2)
         return 0
 
-    lax.fori_loop(0, NB // 4 - 1, two_owners, 0)
-    gather(stage_b, NB // 2)
-    flush(stage_a, NB // 2 - 1)
+    lax.fori_loop(1, NB // 2, owner, 0)
     last = lax.rem(j + core, NB)
-    blocks = blocks_of(stage_b)
+    blocks = gather(last)
     outgo[last, 1] = blocks[:, LANES:]
     block_to(last, 1).start()
 
@@ -464,8 +456,6 @@
             pltpu.VMEM((LON, LANES), BF16),
             pltpu.VMEM((LON, LANES), BF16),
             pltpu.VMEM((ROWS * LON, LANES), F32),
-            pltpu.VMEM((2, CAP_ROWS, LANES), F32),
-            pltpu.VMEM((2, CAP_ROWS, LANES), F32),
             pltpu.VMEM((SLOT_ROWS, LANES), F32),
             pltpu.VMEM((NB, 2, CAP_ROWS, LANES), BF16),
             pltpu.VMEM((NB, CAP_ROWS, LANES), BF16),

time: 68.6 us -> 64.6 us (0.942)
  Pallas kernels: 65.8 us -> 61.8 us
    pallas_call x1, Pallas kernels: 65.8 us -> 61.8 us  [whole(): pl.pallas_call(whole_kernel, out_shape=jax.ShapeDtypeStruct((CB, back.sha...]
where the time goes in v7:
time: 64.6 us; the launch traced here: 64.5 us
  Pallas kernels  61.8 us (96%)
  local copies, waits for them, and re-layouts  2.4 us (4%)
    pallas_call x1, Pallas kernels, whole(): pl.pallas_call(whole_kernel, out_shape=jax.ShapeDtypeStruct((CB, back.sha...  61.8 us
    unnamed x1, local copies, waits for them, and re-layouts  1.79 us

profile of v7, /device:TPU:32, one launch (start us, length us, event | category | flops | bytes accessed | tf_op | source)
XLA Modules:
  0.0 64.5 jit_solution(9330156144446682034)
XLA Ops:
  0.0 0.1 fusion.11
  0.1 0.1 divide_select_fusion
  0.2 0.6 stack.10.coef_ref
  0.8 61.8 %propagate_and_return.1 = bf16[9,13120]{1,0:T(8,128)(2,1)} custom-call(bf16[225,1152]{1,0:T(8,128)(2,1)} %x_ref.1, s32[8,3600]{1,0:T(8,128)} %mask_ref.1, f32[8,128]{1,0:T(8,128)} %stack.10.coef_ref, s32[1,16,1280]{2,1,0:T(8,128)} %cell_ref.1, s32[16,16]{1,0:T(8,128)} %count_ref.1, s32[1,13120]{1,0:T(1,128)} %back_ref.1), custom_call_target="tpu_custom_call" | custom-call | tf_op jit(solution)/shard_map/propagate_and_return/pallas_call | solution.py:434
  62.7 1.8 %copy.7 = bf16[9,13120]{1,0:T(8,128)(2,1)} copy(bf16[9,13120]{1,0:T(8,128)(2,1)} %propagate_and_return.1) | data formatting | bytes 472320
  (2 shorter events, 0.0 us)

commit v8 on v7

--- a/solution.py
+++ b/solution.py
@@ -329,30 +329,40 @@
             comp=c - core + n, pts=d,
         )
 
-    def gather(d):
-        def rows(q, _):
-            base = d * CELLS + q * unroll
-            to = q * unroll + (q // 2) * (CAP_ROWS - USED_ROWS)
-            for u in range(unroll):
-                at = cells.at[pl.ds(base + u, (PAIR_GROUPS - 1) * stride + 1)]
-                stage[pl.ds(to + u, 1), :] = merge_rows(tab, at, PAIR_GROUPS, stride, lane, 2 * CB)
-            return 0
-
-        lax.fori_loop(0, 4, rows, 0)
+    def owner_of(s):
+        return lax.rem(j + 2 * lax.rem(s, NB // 2) + core, NB)
+
+    def pick(d, r, to):
+        at = cells.at[pl.ds(d * CELLS + r, (PAIR_GROUPS - 1) * stride + 1)]
+        stage[pl.ds(to, 1), :] = merge_rows(tab, at, PAIR_GROUPS, stride, lane, 2 * CB)
+
+    def blocks_of():
         packed = jnp.concatenate([stage[0:CAP_ROWS, :], stage[CAP_ROWS : 2 * CAP_ROWS, :]], axis=1)
         return mm(packed.astype(BF16), cut).astype(BF16)
 
+    def first_rows(q, _):
+        for u in range(unroll):
+            r = q * unroll + u
+            pick(owner_of(1), r, r + (q // 2) * (CAP_ROWS - USED_ROWS))
+        return 0
+
+    lax.fori_loop(0, 4, first_rows, 0)
+
     def owner(s, _):
-        d = lax.rem(j + 2 * s + core, NB)
-        blocks = gather(d)
+        before = owner_of(s - 1)
+        blocks = blocks_of()
+        for r in range(USED_ROWS):
+            pick(owner_of(s), r, r)
         for n in range(2):
-            outgo[d, n] = blocks[:, n * LANES : (n + 1) * LANES]
-            block_to(d, n).start()
+            outgo[before, n] = blocks[:, n * LANES : (n + 1) * LANES]
+            block_to(before, n).start()
+        for r in range(USED_ROWS):
+            pick(owner_of(s), USED_ROWS + r, CAP_ROWS + r)
         return 0
 
-    lax.fori_loop(1, NB // 2, owner, 0)
-    last = lax.rem(j + core, NB)
-    blocks = gather(last)
+    lax.fori_loop(2, NB // 2 + 1, owner, 0)
+    last = owner_of(NB // 2)
+    blocks = blocks_of()
     outgo[last, 1] = blocks[:, LANES:]
     block_to(last, 1).start()
 

time: 64.6 us -> 63.7 us (0.986)
  Pallas kernels: 61.8 us -> 60.9 us
    pallas_call x1, Pallas kernels: 61.8 us -> 60.9 us  [whole(): pl.pallas_call(whole_kernel, out_shape=jax.ShapeDtypeStruct((CB, back.sha...]
where the time goes in v8:
time: 63.7 us; the launch traced here: 63.5 us
  Pallas kernels  60.9 us (96%)
  local copies, waits for them, and re-layouts  2.4 us (4%)
    pallas_call x1, Pallas kernels, whole(): pl.pallas_call(whole_kernel, out_shape=jax.ShapeDtypeStruct((CB, back.sha...  60.9 us
    unnamed x1, local copies, waits for them, and re-layouts  1.79 us

profile of v8, /device:TPU:32, one launch (start us, length us, event | category | flops | bytes accessed | tf_op | source)
XLA Modules:
  0.0 63.5 jit_solution(11016399453789262542)
XLA Ops:
  0.0 0.1 fusion.11
  0.1 0.1 divide_select_fusion
  0.2 0.6 stack.10.coef_ref
  0.8 60.9 %propagate_and_return.1 = bf16[9,13120]{1,0:T(8,128)(2,1)} custom-call(bf16[225,1152]{1,0:T(8,128)(2,1)} %x_ref.1, s32[8,3600]{1,0:T(8,128)} %mask_ref.1, f32[8,128]{1,0:T(8,128)} %stack.10.coef_ref, s32[1,16,1280]{2,1,0:T(8,128)} %cell_ref.1, s32[16,16]{1,0:T(8,128)} %count_ref.1, s32[1,13120]{1,0:T(1,128)} %back_ref.1), custom_call_target="tpu_custom_call" | custom-call | tf_op jit(solution)/shard_map/propagate_and_return/pallas_call | solution.py:444
  61.7 1.8 %copy.7 = bf16[9,13120]{1,0:T(8,128)(2,1)} copy(bf16[9,13120]{1,0:T(8,128)(2,1)} %propagate_and_return.1) | data formatting | bytes 472320
  (2 shorter events, 0.0 us)
